TPU v7x, 256 devices: a whole 4x4x8 slice. The times are simulated.
256 devices in a mesh: context: 32 (over x, z), tensor: 8 (over y, core).
Axes of the slice: x: 4, y: 4, z: 8, core: 2. Of those that a mesh axis runs over, the one named last changes fastest.
Arguments:
- first_input: bfloat16 [16, 5376], P(None, 'context'), may hold values from -13 to 13
- second_input: bfloat16 [16, 5376], P(None, 'context'), may hold values from -13 to 13
- attn_gain: bfloat16 [5376], P('context'), may hold values from 0.099609375 to 1.8984375
- query_weight: bfloat16 [5376, 4096], P('context', 'tensor'), may hold values from -0.078125 to 0.078125
- key_weight: bfloat16 [5376, 2048], P('context', 'tensor'), may hold values from -0.25 to 0.25
- value_weight: bfloat16 [5376, 2048], P('context', 'tensor'), may hold values from -0.078125 to 0.078125
- out_weight: bfloat16 [4096, 5376], P('tensor', 'context'), may hold values from -0.09375 to 0.09375
- ffn_gain: bfloat16 [5376], P('context'), may hold values from 0.099609375 to 1.8984375
- gate_weight: bfloat16 [5376, 21504], P('context', 'tensor'), may hold values from -0.078125 to 0.078125
- up_weight: bfloat16 [5376, 21504], P('context', 'tensor'), may hold values from -0.078125 to 0.078125
- down_weight: bfloat16 [21504, 5376], P('tensor', 'context'), may hold values from -0.0625 to 0.0625
- key_cache: bfloat16 [16, 16384, 16, 128], P(None, 'context', 'tensor'), may hold values from -320 to 320
- value_cache: bfloat16 [16, 16384, 16, 128], P(None, 'context', 'tensor'), may hold values from -6 to 6
- lengths: int32 [16], replicated, may hold values from 1 to 16384, as said below
- granularity: int32 [16], replicated, may hold values from 1 to 8, as said below
Outputs:
- first_output: bfloat16 [16, 5376], P(None, 'context')
- second_output: bfloat16 [16, 5376], P(None, 'context')
Inputs may be any that keep to these rules, and one draw needn't show every extreme that they name: `lengths`: some request has all 16384 positions live. `granularity`: some request uses all 8 granularities.
All inputs are finite; a program needn't handle non-finite values.
Results may differ from a plain program's by a relative error of at most 0.0118.
Values may be sent and summed in bfloat16 or wider, within the bound.
A program may use at most 64 MiB of HBM per device.

v0:
```python
import jax
import jax.numpy as jnp
from jax import lax
from jax.sharding import PartitionSpec as P

LEVELS = 8


EPS = 1e-06
MASKED = -1e30


def decode_step(inputs, earlier, params):
    (
        attn_gain,
        query_weight,
        key_weight,
        value_weight,
        out_weight,
        ffn_gain,
        gate_weight,
        up_weight,
        down_weight,
        key_cache,
        value_cache,
        lengths,
        granularity,
    ) = params
    requests = inputs.shape[0]
    model_width = inputs.shape[1] * lax.axis_size("context")
    head_size = key_cache.shape[3]
    kv_local = key_cache.shape[2]
    heads_local = query_weight.shape[1] // head_size
    group_size = heads_local // kv_local
    positions_local = key_cache.shape[1]
    score_scale = head_size ** (-0.5)
    rows_f32 = inputs.astype(jnp.float32)
    gated = (rows_f32 * attn_gain.astype(jnp.float32)).astype(jnp.bfloat16)
    query_part = jnp.dot(gated, query_weight, preferred_element_type=jnp.float32)
    key_part = jnp.dot(gated, key_weight, preferred_element_type=jnp.float32)
    value_part = jnp.dot(gated, value_weight, preferred_element_type=jnp.float32)
    square_part = jnp.sum(rows_f32 * rows_f32, axis=1)
    query_sum, key_sum, value_sum, square_sum = lax.psum(
        (query_part, key_part, value_part, square_part), "context"
    )
    row_inv = lax.rsqrt(square_sum / model_width + EPS)[:, None]
    queries = (
        (query_sum * row_inv)
        .astype(jnp.bfloat16)
        .reshape(requests, kv_local, group_size, head_size)
    )
    new_key = (key_sum * row_inv).astype(jnp.bfloat16).reshape(requests, kv_local, head_size)
    new_value = (value_sum * row_inv).astype(jnp.bfloat16).reshape(requests, kv_local, head_size)
    extras = earlier + [(new_key, new_value)]
    first_pos = lax.axis_index("context") * positions_local
    positions = first_pos + jnp.arange(positions_local, dtype=jnp.int32)
    live_keys = (positions[None, :] < lengths[:, None])[:, None, None, :]
    scores = (
        jnp.einsum("rkge,rpke->rkgp", queries, key_cache, preferred_element_type=jnp.float32)
        * score_scale
    )
    local_peak = jnp.max(jnp.where(live_keys, scores, MASKED), axis=3)
    weights = jnp.where(live_keys, jnp.exp(scores - local_peak[..., None]), 0.0)
    totals = jnp.sum(weights, axis=3)
    mixture = jnp.einsum(
        "rkgp,rpke->rkge",
        weights.astype(jnp.bfloat16),
        value_cache,
        preferred_element_type=jnp.float32,
    )
    cache_peak = lax.pmax(local_peak, "context")
    rescale = jnp.exp(local_peak - cache_peak)
    cache_total, cache_mix = lax.psum((totals * rescale, mixture * rescale[..., None]), "context")
    own_list = [
        jnp.einsum("rkge,rke->rkg", queries, pair_item[0], preferred_element_type=jnp.float32)
        * score_scale
        for pair_item in extras
    ]
    highest = cache_peak
    for own_score in own_list:
        highest = jnp.maximum(highest, own_score)
    cache_scale = jnp.exp(cache_peak - highest)
    denominator = cache_total * cache_scale
    numerator = cache_mix * cache_scale[..., None]
    for own_score, pair_item in zip(own_list, extras):
        own_weight = jnp.exp(own_score - highest)
        denominator = denominator + own_weight
        numerator = (
            numerator + own_weight[..., None] * pair_item[1].astype(jnp.float32)[:, :, None, :]
        )
    attended = (
        (numerator / denominator[..., None])
        .astype(jnp.bfloat16)
        .reshape(requests, heads_local * head_size)
    )
    out_part = jnp.dot(attended, out_weight, preferred_element_type=jnp.float32)
    residual = rows_f32 + lax.psum(out_part, "tensor")
    ffn_gated = (residual * ffn_gain.astype(jnp.float32)).astype(jnp.bfloat16)
    ffn_square_part = jnp.sum(residual * residual, axis=1)
    gate_part = jnp.dot(ffn_gated, gate_weight, preferred_element_type=jnp.float32)
    up_part = jnp.dot(ffn_gated, up_weight, preferred_element_type=jnp.float32)
    ffn_local = gate_weight.shape[1]
    level_cols = ffn_local * lax.axis_size("tensor") // LEVELS
    columns = lax.axis_index("tensor") * ffn_local + jnp.arange(ffn_local, dtype=jnp.int32)
    active = columns[None, :] < granularity[:, None] * level_cols
    gate_sum, up_sum, ffn_square = lax.psum((gate_part, up_part, ffn_square_part), "context")
    ffn_inv = lax.rsqrt(ffn_square / model_width + EPS)[:, None]
    gate_sum = gate_sum * ffn_inv
    up_sum = up_sum * ffn_inv
    hidden = jnp.where(active, jax.nn.gelu(gate_sum, approximate=True) * up_sum, 0.0).astype(
        jnp.bfloat16
    )
    down_part = jnp.dot(hidden, down_weight, preferred_element_type=jnp.float32)
    output = (residual + lax.psum(down_part, "tensor")).astype(jnp.bfloat16)
    return (output, extras)


def per_device(
    first_input,
    second_input,
    attn_gain,
    query_weight,
    key_weight,
    value_weight,
    out_weight,
    ffn_gain,
    gate_weight,
    up_weight,
    down_weight,
    key_cache,
    value_cache,
    lengths,
    granularity,
):
    params = (
        attn_gain,
        query_weight,
        key_weight,
        value_weight,
        out_weight,
        ffn_gain,
        gate_weight,
        up_weight,
        down_weight,
        key_cache,
        value_cache,
        lengths,
        granularity,
    )
    first_output, extras = decode_step(first_input, [], params)
    second_output, unused_extras = decode_step(second_input, extras, params)
    return (first_output, second_output)


def solution(mesh):
    return jax.shard_map(
        per_device,
        mesh=mesh,
        in_specs=(
            P(None, "context"),
            P(None, "context"),
            P("context"),
            P("context", "tensor"),
            P("context", "tensor"),
            P("context", "tensor"),
            P("tensor", "context"),
            P("context"),
            P("context", "tensor"),
            P("context", "tensor"),
            P("tensor", "context"),
            P(None, "context", "tensor", None),
            P(None, "context", "tensor", None),
            P(),
            P(),
        ),
        out_specs=(P(None, "context"), P(None, "context")),
        check_vma=False,
    )
```

profile of v0, /device:TPU:1, one launch (start us, length us, event | category | flops | bytes accessed | tf_op | source)
XLA Modules:
  0.0 658.3 jit_solution(4174749539116453880)
XLA Ops:
  8.0 1.3 fusion.67
  9.3 1.7 fusion.82
  10.9 1.7 fusion.76
  12.6 1.3 fusion.69
  14.0 1.7 fusion.72
  15.7 1.6 fusion.78
  17.3 1.6 fusion.74
  19.0 1.6 fusion.80
  21.3 131.7 %all-reduce.13.cloned.1.call-done = (f32[16,512]{1,0:T(8,128)}, f32[16]{0:T(128)}, f32[16,512]{1,0:T(8,128)}, f32[16]{0:T(128)}) async-done(((f32[16,512]{1,0:T(8,128)}, f32[16]{0:T(128)}, f32[16,512]{1,0:T(8,128)}, f32[16]{0:T(128)}), (f32[16,512]{1,0:T(8,128)}, f32[16]{0:T(128)}, f32[16,512]{1,0:T(8,128)}, f32[16]{0:T(128)})) %all-reduce.13.cloned.1.call-update) | async-done | bytes 65680 | tf_op jit(solution)/shard_map/psum | solution.py:43
  155.3 3.5 fusion.8
  158.8 1.4 select_reduce_fusion
  160.2 113.2 %all-reduce.4 = (f32[16,2,2]{2,1,0:T(2,128)S(1)}, f32[16,2,2]{2,1,0:T(2,128)S(1)}) all-reduce(f32[16,2,2]{2,1,0:T(2,128)S(1)} %get-tuple-element.5, f32[16,2,2]{2,1,0:T(2,128)S(1)} %get-tuple-element.4), channel_id=1, replica_groups=mesh['context'=32,'tensor'=8] {'context'}, use_global_device_ids=true, to_apply=%region_4.0 | all-reduce | flops 128 | bytes 1024 | tf_op jit(solution)/shard_map/pmax | solution.py:71
  274.5 3.8 fusion.17
  278.9 1.3 fusion.14
  280.3 164.8 %all-reduce.11.cloned.1.call-done = (f32[16,2,2,128]{3,2,1,0:T(2,128)}, f32[16,256]{1,0:T(8,128)}, f32[16,2,2]{2,1,0:T(2,128)}, f32[16,256]{1,0:T(8,128)}, f32[1...) async-done(((f32[16,2,2,128]{3,2,1,0:T(2,128)}, f32[16,256]{1,0:T(8,128)}, f32[16,2,2]{2,1,0:T(2,128)}, f32[16,256]{1,0:T(8,128)}, ...) | async-done | bytes 131600 | tf_op jit(solution)/shard_map/psum | solution.py:73
  448.8 1.1 fusion.61
  450.2 25.4 %all-reduce.6 = (f32[16,168]{1,0:T(8,128)S(1)}, f32[16,168]{1,0:T(8,128)S(1)}) all-reduce(f32[16,168]{1,0:T(8,128)S(1)} %fusion.101, f32[16,168]{1,0:T(8,128)S(1)} %fusion.106), channel_id=1, replica_groups=mesh['context'=32,'tensor'=8] {'tensor'}, use_global_device_ids=true, to_apply=%region_10.11 | all-reduce | flops 5376 | bytes 43008 | tf_op jit(solution)/shard_map/psum | solution.py:97
  476.8 0.9 fusion.103
  478.6 0.9 fusion.108
  479.6 58.4 %all-reduce = (f32[16]{0:T(128)S(1)}, f32[16]{0:T(128)S(1)}) all-reduce(f32[16]{0:T(128)S(1)} %get-tuple-element.43, f32[16]{0:T(128)S(1)} %get-tuple-element.41), channel_id=1, replica_groups=mesh['context'=32,'tensor'=8] {'context'}, use_global_device_ids=true, to_apply=%region_13.14 | all-reduce | flops 32 | bytes 256 | tf_op jit(solution)/shard_map/psum | solution.py:106
  538.1 84.0 %all-reduce.15.cloned.1.call-done = (f32[16,2688]{1,0:T(8,128)}, f32[16,2688]{1,0:T(8,128)}, f32[16,2688]{1,0:T(8,128)}, f32[16,2688]{1,0:T(8,128)}) async-done(((f32[16,2688]{1,0:T(8,128)}, f32[16,2688]{1,0:T(8,128)}, f32[16,2688]{1,0:T(8,128)}, f32[16,2688]{1,0:T(8,128)}), (f32[16,2688]{1,0:T(8,128)}, f32[16,2688]{1,0:T(8,128)}, f32[16,2688]{1,0:T(8,128)}, ...) | async-done | bytes 688144 | tf_op jit(solution)/shard_map/psum | solution.py:106
  622.1 1.4 fusion.38
  623.5 1.4 fusion.40
  624.9 25.6 %all-reduce.5 = (f32[16,168]{1,0:T(8,128)S(1)}, f32[16,168]{1,0:T(8,128)S(1)}) all-reduce(f32[16,168]{1,0:T(8,128)S(1)} %fusion.40, f32[16,168]{1,0:T(8,128)S(1)} %fusion.38), channel_id=1, replica_groups=mesh['context'=32,'tensor'=8] {'tensor'}, use_global_device_ids=true, to_apply=%region_15.16 | all-reduce | flops 5376 | bytes 43008 | tf_op jit(solution)/shard_map/psum | solution.py:114
  (63 shorter events, 12.8 us)
Async XLA Ops:
  7.2 468.7 %copy-start = (bf16[168,2688]{1,0:T(8,128)(2,1)S(1)}, bf16[168,2688]{1,0:T(8,128)(2,1)}, u32[]{:S(2)}) copy-start(bf16[168,2688]{1,0:T(8,128)(2,1)} %param.23) | copy-start | bytes 2709508
  7.2 145.9 %all-reduce.13.cloned.1.call-start = ((), (), s32[]{:S(2)}) async-start(), calls=%async_computation.1 | async-start | bytes 133120 | tf_op jit(solution)/shard_map/psum | solution.py:43
  14.0 431.1 %all-reduce.11.cloned.1.call-start = ((), (), s32[]{:S(2)}) async-start(), calls=%async_computation | async-start | bytes 327680 | tf_op jit(solution)/shard_map/psum | solution.py:73
  155.3 3.5 copy-start.1
  273.4 5.5 copy-start.7
  274.5 5.8 copy-start.8
  278.2 171.6 %copy-start.4 = (bf16[512,168]{0,1:T(8,128)(2,1)S(1)}, bf16[512,168]{0,1:T(8,128)(2,1)}, u32[]{:S(2)}) copy-start(bf16[512,168]{0,1:T(8,128)(2,1)} %param.21) | copy-start | bytes 516100
  278.2 197.4 %copy-start.5 = (bf16[16,168]{1,0:T(8,128)(2,1)S(1)}, bf16[16,168]{1,0:T(8,128)(2,1)}, u32[]{:S(2)}) copy-start(bf16[16,168]{1,0:T(8,128)(2,1)} %param.16) | copy-start | bytes 16132
  278.2 197.5 %copy-start.6 = (bf16[16,168]{1,0:T(8,128)(2,1)S(1)}, bf16[16,168]{1,0:T(8,128)(2,1)}, u32[]{:S(2)}) copy-start(bf16[16,168]{1,0:T(8,128)(2,1)} %param.15) | copy-start | bytes 16132
  278.2 198.5 %copy-start.2 = (bf16[168,2688]{1,0:T(8,128)(2,1)S(1)}, bf16[168,2688]{1,0:T(8,128)(2,1)}, u32[]{:S(2)}) copy-start(bf16[168,2688]{1,0:T(8,128)(2,1)} %param.24) | copy-start | bytes 2709508
  280.2 199.4 %copy-start.9 = (s32[16]{0:T(128)S(1)}, s32[16]{0:T(128)}, u32[]{:S(2)}) copy-start(s32[16]{0:T(128)} %param.29) | copy-start | bytes 196
  280.2 341.9 %copy-start.3 = (bf16[2688,168]{0,1:T(8,128)(2,1)S(1)}, bf16[2688,168]{0,1:T(8,128)(2,1)}, u32[]{:S(2)}) copy-start(bf16[2688,168]{0,1:T(8,128)(2,1)} %param.25) | copy-start | bytes 2709508
  280.2 341.9 %all-reduce.15.cloned.1.call-start = ((), (), s32[]{:S(2)}) async-start(), calls=%async_computation.2 | async-start | bytes 1376256 | tf_op jit(solution)/shard_map/psum | solution.py:106
Sparse Core Ops, SparseCore 0:
  14.1 138.9 all-reduce.12
  280.4 164.6 all-reduce.10
  479.7 142.3 all-reduce.14
where the time goes:
time: 660 us; the launch traced here: 658 us
  waiting for transfers between devices  381 us (58%)
  blocking collectives  223 us (34%)
  matrix products  27.2 us (4%)
  between operations  13.9 us (2%)
  other arithmetic  13.6 us (2%)
    psum x1, waiting for transfers between devices, decode_step(): lax.psum((totals * rescale, mixture * rescale[..., None]), 'context')  165 us
    psum x1, waiting for transfers between devices, decode_step(): lax.psum((query_part, key_part, value_part, square_part), 'context')  132 us
    pmax x1, blocking collectives, decode_step(): cache_peak = lax.pmax(local_peak, 'context')  113 us
    psum x1, waiting for transfers between devices, decode_step(): lax.psum((gate_part, up_part, ffn_square_part), 'context')  84 us
    psum x1, blocking collectives, decode_step(): lax.psum((gate_part, up_part, ffn_square_part), 'context')  58.4 us
    psum x1, blocking collectives, decode_step(): output = (residual + lax.psum(down_part, 'tensor')).astype(jnp.bfloat16)  25.6 us
    psum x1, blocking collectives, decode_step(): residual = rows_f32 + lax.psum(out_part, 'tensor')  25.4 us
  transfers between devices with their start and end apart: 3, of which 3 were waited for; matrix products, arithmetic and copies ran while one was open for 1% of the time, Pallas kernels for 0%

commit v1 on v0

v1 whole, which is shorter than its diff:
```python
import math

import jax
import jax.numpy as jnp
from jax import lax
from jax.experimental import pallas as pl
from jax.experimental.pallas import tpu as pltpu
from jax.sharding import PartitionSpec as P

EPS = 1e-06
MASKED = -1e30
WIDTH = 5376
COLS = 168
HEAD = 128
CTX = 32
TEN = 8
REQS = 16
ROWS = 32
POS = 512
TILES = 21
EXTRA = 10
SCALE = HEAD**-0.5
GELU = math.sqrt(2.0 / math.pi)
MESH = pl.DeviceIdType.MESH
F32 = jnp.float32
BF16 = jnp.bfloat16

N_LOCAL = 15


def iota(shape, dim):
    return lax.broadcasted_iota(jnp.int32, shape, dim)


def peer_of(x, z, i):
    zi, xi = i // 4, i % 4
    zo = 4 + ((zi + 1) // 2) * (1 - 2 * (zi % 2))
    xo = 2 + ((xi + 1) // 2) * (1 - 2 * (xi % 2))
    return lax.rem(x + xo, 4) * 8 + lax.rem(z + zo, 8)


def nt_dot(a, b):
    return lax.dot_general(a, b, (((1,), (1,)), ((), ())), preferred_element_type=F32)


def kernel(
    lengths,
    granularity,
    x1_hbm,
    x2_hbm,
    gains_hbm,
    wq_hbm,
    wk_hbm,
    wv_hbm,
    wo_hbm,
    wg_hbm,
    wu_hbm,
    wd_hbm,
    kc_hbm,
    vc_hbm,
    o1_ref,
    o2_ref,
    x1,
    x2,
    gains,
    wq,
    wk,
    wv,
    wo,
    wg,
    wu,
    wd,
    kc,
    vc,
    qkv_out,
    qkv_in,
    qkv_all,
    mix_out,
    mix_in,
    att_all,
    proj_out,
    proj_in,
    sq_out,
    sq_in,
    gu_out,
    gu_in,
    gu_in2,
    hid_all,
    down_in,
    local_sem,
    send_sem,
    recv_sem,
):
    c = lax.axis_index("context")
    t = lax.axis_index("tensor")
    x, z = c // 8, c % 8

    def local(i, src, dst):
        return pltpu.make_async_copy(src, dst, local_sem.at[i])

    loads = [
        local(0, x1_hbm, x1),
        local(1, x2_hbm, x2),
        local(2, gains_hbm, gains),
        local(3, wq_hbm, wq),
        local(4, wk_hbm, wk),
        local(5, wv_hbm, wv),
        local(6, kc_hbm, kc),
        local(7, vc_hbm, vc),
        local(8, wo_hbm, wo),
        local(9, wg_hbm, wg),
        local(10, wu_hbm, wu),
        local(11, wd_hbm, wd),
    ]
    for load in loads:
        load.start()

    barrier = pltpu.get_barrier_semaphore()

    @pl.loop(0, CTX - 1)
    def _(i):
        pl.semaphore_signal(
            barrier, inc=1, device_id=(peer_of(x, z, i), t), device_id_type=MESH
        )

    @pl.loop(1, TEN)
    def _(d):
        pl.semaphore_signal(
            barrier, inc=1, device_id=(c, lax.rem(t + d, TEN)), device_id_type=MESH
        )

    def send(phase, src, dst, peer):
        pltpu.make_async_remote_copy(
            src_ref=src,
            dst_ref=dst,
            send_sem=send_sem.at[phase],
            recv_sem=recv_sem.at[phase],
            device_id=peer,
            device_id_type=MESH,
        ).start()

    def wait(sem, ref):
        pltpu.make_async_copy(ref, ref, sem).wait()

    for i in range(6):
        loads[i].wait()
    rows = jnp.concatenate([x1[...], x2[...]], axis=0).astype(F32)
    gated = (rows * gains[0:1, :]).astype(BF16)
    q_part = jnp.dot(gated, wq[...], preferred_element_type=F32)
    k_part = jnp.dot(gated, wk[...], preferred_element_type=F32)
    v_part = jnp.dot(gated, wv[...], preferred_element_type=F32)
    part = jnp.concatenate([q_part, k_part, v_part], axis=1)
    square = jnp.sum(rows * rows, axis=1, keepdims=True)
    square_hi = square.astype(BF16).astype(F32)
    square_tile = jnp.where(iota((ROWS, HEAD), 1) == 0, square_hi, square - square_hi)
    for j in range(8):
        for g in range(4):
            tile = jnp.concatenate(
                [
                    part[g * 8 : g * 8 + 8, j * HEAD : (j + 1) * HEAD],
                    square_tile[g * 8 : g * 8 + 8, :],
                ],
                axis=0,
            )
            qkv_out[j * 4 + g] = tile.astype(BF16)

    pl.semaphore_wait(barrier, CTX - 1 + TEN - 1)

    @pl.loop(0, CTX - 1)
    def _(i):
        p = peer_of(x, z, i)
        send(0, qkv_out.at[p], qkv_in.at[i], (p, t))

    qkv_in[CTX - 1] = qkv_out[c]
    wait(recv_sem.at[0], qkv_in.at[pl.ds(0, CTX - 1)])
    total = jnp.sum(qkv_in[...].astype(F32), axis=0)
    squares = total[8:16, 0:1] + total[8:16, 1:2]
    inv = lax.rsqrt(squares / WIDTH + EPS)
    mine = pl.multiple_of(c * 8, 8)
    qkv_all[pl.ds(mine, 8), :] = (total[0:8, :] * inv).astype(BF16).astype(F32)

    @pl.loop(0, CTX - 1)
    def _(i):
        tile = qkv_all.at[pl.ds(mine, 8)]
        send(1, tile, tile, (peer_of(x, z, i), t))

    wait(recv_sem.at[1], qkv_all.at[pl.ds(0, 8 * (CTX - 1))])

    loads[6].wait()
    loads[7].wait()
    lane = iota((8, 2 * POS), 1)
    own_head = (lane % 2) == (iota((8, 2 * POS), 0) // 4)
    position = c * POS + lane // 2

    @pl.loop(0, REQS)
    def _(r):
        queries = qkv_all[pl.ds(r, 8, stride=16), :].astype(BF16)
        scores = nt_dot(queries, kc[r]) * SCALE
        live = own_head & (position < lengths[r])
        peak = jnp.max(jnp.where(live, scores, MASKED), axis=1, keepdims=True)
        weights = jnp.where(live, jnp.exp(scores - peak), 0.0)
        sums = jnp.sum(weights, axis=1, keepdims=True)
        mixture = jnp.dot(weights.astype(BF16), vc[r], preferred_element_type=F32)
        stats = jnp.where(iota((8, HEAD), 1) < 64, peak, sums)
        mix_out[2 * r] = jnp.concatenate([mixture[0:4], stats[0:4]], axis=0)
        mix_out[2 * r + 1] = jnp.concatenate([mixture[4:8], stats[4:8]], axis=0)

    @pl.loop(0, CTX - 1)
    def _(i):
        p = peer_of(x, z, i)
        send(2, mix_out.at[p], mix_in.at[i], (p, t))

    mix_in[CTX - 1] = mix_out[c]
    request, kv = c // 2, c % 2

    def new_row(j, s):
        return qkv_all[pl.ds(j * 32 + s * 16 + request, 1), :]

    query = jnp.concatenate([new_row(2 * kv + m // 2, m % 2) for m in range(4)], axis=0)
    own = [
        jnp.sum(query * new_row(4 + kv, s), axis=1, keepdims=True) * SCALE for s in range(2)
    ]
    second = (iota((4, 1), 0) % 2) == 1
    own[1] = jnp.where(second, own[1], MASKED)
    wait(recv_sem.at[2], mix_in.at[pl.ds(0, CTX - 1)])
    mixed = mix_in[:, 0:4, :]
    peaks = mix_in[:, 4:8, 0:1]
    sums = mix_in[:, 4:8, 64:65]
    highest = jnp.maximum(jnp.max(peaks, axis=0), jnp.maximum(own[0], own[1]))
    rescale = jnp.exp(peaks - highest[None])
    denominator = jnp.sum(rescale * sums, axis=0)
    numerator = jnp.sum(rescale * mixed, axis=0)
    own_weight = [jnp.exp(own[0] - highest), jnp.where(second, jnp.exp(own[1] - highest), 0.0)]
    for s in range(2):
        denominator = denominator + own_weight[s]
        numerator = numerator + own_weight[s] * new_row(6 + kv, s)
    attended = (numerator / denominator).astype(BF16).astype(F32)
    att_all[pl.ds(mine, 8), :] = jnp.concatenate([attended, attended], axis=0)

    @pl.loop(0, CTX - 1)
    def _(i):
        tile = att_all.at[pl.ds(mine, 8)]
        send(3, tile, tile, (peer_of(x, z, i), t))

    loads[8].wait()
    wait(recv_sem.at[3], att_all.at[pl.ds(0, 8 * (CTX - 1))])

    att = jnp.concatenate(
        [
            jnp.concatenate(
                [
                    att_all[pl.ds((j // 2) * 8 + (j % 2) * 2 + s, REQS, stride=16), :]
                    for s in range(2)
                ],
                axis=0,
            )
            for j in range(4)
        ],
        axis=1,
    ).astype(BF16)
    pad = jnp.zeros((ROWS, 2 * HEAD - COLS), F32)

    def over_tensor(phase, value, slots):
        proj_out[phase - 4] = jnp.concatenate([value, pad], axis=1).astype(BF16)

        @pl.loop(1, TEN)
        def _(d):
            send(phase, proj_out.at[phase - 4], slots.at[t], (c, lax.rem(t + d, TEN)))

        slots[t] = proj_out[phase - 4]
        wait(recv_sem.at[phase], slots.at[pl.ds(0, TEN - 1)])
        return jnp.sum(slots[...].astype(F32), axis=0)[:, 0:COLS]

    residual = rows + over_tensor(4, nt_dot(att, wo[...]), proj_in)

    square = jnp.sum(residual * residual, axis=1, keepdims=True)
    diagonal = iota((ROWS, HEAD), 0) == iota((ROWS, HEAD), 1)
    sq_out[...] = jnp.sum(jnp.where(diagonal, square, 0.0), axis=0, keepdims=True)

    @pl.loop(0, CTX - 1)
    def _(i):
        send(6, sq_out, sq_in.at[i], (peer_of(x, z, i), t))

    sq_in[CTX - 1] = sq_out[...]
    ffn_gated = (residual * gains[1:2, :]).astype(BF16)
    loads[9].wait()
    loads[10].wait()

    @pl.loop(0, 7)
    def _(n):
        columns = pl.ds(pl.multiple_of(n * 384, 384), 384)
        gate = jnp.dot(ffn_gated, wg[:, columns], preferred_element_type=F32).astype(BF16)
        up = jnp.dot(ffn_gated, wu[:, columns], preferred_element_type=F32).astype(BF16)
        for k in range(3):
            for s in range(2):
                unit = 6 * n + 2 * k + s
                gu_out[unit, 0:16, :] = gate[s * 16 : s * 16 + 16, k * HEAD : (k + 1) * HEAD]
                gu_out[unit, 16:32, :] = up[s * 16 : s * 16 + 16, k * HEAD : (k + 1) * HEAD]

    @pl.loop(0, CTX - 1)
    def _(i):
        p = peer_of(x, z, i)
        send(7, gu_out.at[p], gu_in.at[i], (p, t))

    @pl.loop(0, EXTRA)
    def _(p):
        @pl.when(p != c)
        def _():
            send(8, gu_out.at[CTX + p], gu_in2.at[c], (p, t))

    gu_in[CTX - 1] = gu_out[c]

    wait(recv_sem.at[6], sq_in.at[pl.ds(0, CTX - 1)])
    squares = jnp.sum(sq_in[...], axis=0)
    step_rows = iota((REQS, HEAD), 1) == iota((REQS, HEAD), 0) + REQS * (c % 2)
    squares = jnp.sum(jnp.where(step_rows, squares, 0.0), axis=1, keepdims=True)
    ffn_inv = lax.rsqrt(squares / WIDTH + EPS)
    levels = jnp.zeros((REQS, 1), jnp.int32)
    for r in range(REQS):
        levels = jnp.where(iota((REQS, 1), 0) == r, granularity[r], levels)
    active = levels > t

    def hidden_of(slots):
        both = jnp.sum(slots[...].astype(F32), axis=0)
        gate = both[0:16] * ffn_inv
        up = both[16:32] * ffn_inv
        act = 0.5 * gate * (1.0 + jnp.tanh(GELU * (gate + 0.044715 * (gate * gate * gate))))
        return jnp.where(active, act * up, 0.0).astype(BF16)

    def share(phase, unit):
        part_of = hid_all.at[pl.ds(pl.multiple_of(unit * 16, 16), 16)]

        @pl.loop(0, CTX - 1)
        def _(i):
            send(phase, part_of, part_of, (peer_of(x, z, i), t))

    wait(recv_sem.at[7], gu_in.at[pl.ds(0, CTX - 1)])
    hid_all[pl.ds(pl.multiple_of(c * 16, 16), 16), :] = hidden_of(gu_in)
    share(9, c)

    @pl.when(c < EXTRA)
    def _():
        gu_in2[c] = gu_out[CTX + c]
        wait(recv_sem.at[8], gu_in2.at[pl.ds(0, CTX - 1)])
        hid_all[pl.ds(pl.multiple_of((CTX + c) * 16, 16), 16), :] = hidden_of(gu_in2)
        share(10, CTX + c)

    loads[11].wait()
    wait(recv_sem.at[9], hid_all.at[pl.ds(0, 16 * (CTX - 1))])

    @pl.when(c < EXTRA)
    def _():
        wait(recv_sem.at[10], hid_all.at[pl.ds(0, 16 * (EXTRA - 1))])

    @pl.when(c >= EXTRA)
    def _():
        wait(recv_sem.at[10], hid_all.at[pl.ds(0, 16 * EXTRA)])

    hidden = jnp.concatenate(
        [hid_all[i * ROWS : (i + 1) * ROWS, :] for i in range(TILES)], axis=1
    )
    output = residual + over_tensor(5, nt_dot(hidden, wd[...]), down_in)
    output = output.astype(BF16)
    o1_ref[...] = output[0:REQS]
    o2_ref[...] = output[REQS:ROWS]

    wait(send_sem.at[0], qkv_in.at[pl.ds(0, CTX - 1)])
    wait(send_sem.at[1], qkv_all.at[pl.ds(0, 8 * (CTX - 1))])
    wait(send_sem.at[2], mix_in.at[pl.ds(0, CTX - 1)])
    wait(send_sem.at[3], att_all.at[pl.ds(0, 8 * (CTX - 1))])
    wait(send_sem.at[4], proj_in.at[pl.ds(0, TEN - 1)])
    wait(send_sem.at[5], down_in.at[pl.ds(0, TEN - 1)])
    wait(send_sem.at[6], sq_in.at[pl.ds(0, CTX - 1)])
    wait(send_sem.at[7], gu_in.at[pl.ds(0, CTX - 1)])

    wait(send_sem.at[9], hid_all.at[pl.ds(0, 16 * (CTX - 1))])

    @pl.when(c < EXTRA)
    def _():
        wait(send_sem.at[8], gu_in.at[pl.ds(0, EXTRA - 1)])
        wait(send_sem.at[10], hid_all.at[pl.ds(0, 16 * (CTX - 1))])

    @pl.when(c >= EXTRA)
    def _():
        wait(send_sem.at[8], gu_in.at[pl.ds(0, EXTRA)])


def per_device(
    first_input,
    second_input,
    attn_gain,
    query_weight,
    key_weight,
    value_weight,
    out_weight,
    ffn_gain,
    gate_weight,
    up_weight,
    down_weight,
    key_cache,
    value_cache,
    lengths,
    granularity,
):
    gains = jnp.stack([attn_gain, ffn_gain]).astype(F32)
    any_space = pl.BlockSpec(memory_space=pl.ANY)
    smem = pl.BlockSpec(memory_space=pltpu.SMEM)
    vmem = pl.BlockSpec(memory_space=pltpu.VMEM)
    V = pltpu.VMEM
    return pl.pallas_call(
        kernel,
        out_shape=(
            jax.ShapeDtypeStruct((REQS, COLS), BF16),
            jax.ShapeDtypeStruct((REQS, COLS), BF16),
        ),
        in_specs=[smem, smem] + [any_space] * 12,
        out_specs=(vmem, vmem),
        scratch_shapes=[
            V((REQS, COLS), BF16),
            V((REQS, COLS), BF16),
            V((2, COLS), F32),
            V((COLS, 512), BF16),
            V((COLS, 256), BF16),
            V((COLS, 256), BF16),
            V((COLS, 512), BF16),
            V((COLS, 2688), BF16),
            V((COLS, 2688), BF16),
            V((COLS, 2688), BF16),
            V((REQS, 2 * POS, HEAD), BF16),
            V((REQS, 2 * POS, HEAD), BF16),
            V((CTX, 16, HEAD), BF16),
            V((CTX, 16, HEAD), BF16),
            V((CTX * 8, HEAD), F32),
            V((CTX, 8, HEAD), F32),
            V((CTX, 8, HEAD), F32),
            V((CTX * 8, HEAD), F32),
            V((2, ROWS, 2 * HEAD), BF16),
            V((TEN, ROWS, 2 * HEAD), BF16),
            V((1, HEAD), F32),
            V((CTX, 1, HEAD), F32),
            V((2 * TILES, 32, HEAD), BF16),
            V((CTX, 32, HEAD), BF16),
            V((CTX, 32, HEAD), BF16),
            V((TILES * ROWS, HEAD), BF16),
            V((TEN, ROWS, 2 * HEAD), BF16),
            pltpu.SemaphoreType.DMA((12,)),
            pltpu.SemaphoreType.DMA((11,)),
            pltpu.SemaphoreType.DMA((11,)),
        ],
        compiler_params=pltpu.CompilerParams(
            collective_id=0, has_side_effects=True, vmem_limit_bytes=40 * 2**20
        ),
    )(
        lengths,
        granularity,
        first_input,
        second_input,
        gains,
        query_weight,
        key_weight,
        value_weight,
        out_weight.T,
        gate_weight,
        up_weight,
        down_weight.T,
        key_cache.reshape(REQS, 2 * POS, HEAD),
        value_cache.reshape(REQS, 2 * POS, HEAD),
    )


def solution(mesh):
    return jax.shard_map(
        per_device,
        mesh=mesh,
        in_specs=(
            P(None, "context"),
            P(None, "context"),
            P("context"),
            P("context", "tensor"),
            P("context", "tensor"),
            P("context", "tensor"),
            P("tensor", "context"),
            P("context"),
            P("context", "tensor"),
            P("context", "tensor"),
            P("tensor", "context"),
            P(None, "context", "tensor", None),
            P(None, "context", "tensor", None),
            P(),
            P(),
        ),
        out_specs=(P(None, "context"), P(None, "context")),
        check_vma=False,
    )
```

time: 660 us -> 90.8 us (0.14)
  waiting for transfers between devices: 381 us -> 0 us
  blocking collectives: 223 us -> 0 us
  Pallas kernels: 0 us -> 72.9 us
  matrix products: 27.2 us -> 0 us
  local copies, waits for them, and re-layouts: 0.16 us -> 16.7 us
  other arithmetic: 13.6 us -> 0.01 us
  between operations: 13.9 us -> 0.66 us
    psum x3 -> x0, waiting for transfers between devices: 381 us -> none  [the longest x1 165 us: decode_step(): lax.psum((totals * rescale, mixture * rescale[..., None]), 'context')]
    pmax x1 -> x0, blocking collectives: 113 us -> none  [decode_step(): cache_peak = lax.pmax(local_peak, 'context')]
    psum x3 -> x0, blocking collectives: 109 us -> none  [the longest x1 58.4 us: decode_step(): lax.psum((gate_part, up_part, ffn_square_part), 'context')]
    pallas_call x0 -> x1, Pallas kernels: none -> 72.9 us  [per_device(): pl.pallas_call(kernel, out_shape=(jax.ShapeDtypeStruct((REQS, COLS), BF16...]
    dot_general x21 -> x0, matrix products: 27.2 us -> none  [the longest x2 5.11 us: decode_step(): jnp.einsum('rkgp,rpke->rkge', weights.astype(jnp.bfloat16), value_cache,...]
    unnamed x20 -> x28, local copies, waits for them, and re-layouts: 0.05 us -> 15.4 us
  transfers between devices with their start and end apart: 3 -> 0, of which waited for: 3 -> 0; matrix products, arithmetic and copies ran while one was open for 1% -> 0% of each run, Pallas kernels for 0% -> 0%
where the time goes in v1:
time: 90.8 us; the launch traced here: 90.3 us
  Pallas kernels  72.9 us (80%)
  local copies, waits for them, and re-layouts  16.7 us (18%)
    pallas_call x1, Pallas kernels, per_device(): pl.pallas_call(kernel, out_shape=(jax.ShapeDtypeStruct((REQS, COLS), BF16...  72.9 us
    unnamed x28, local copies, waits for them, and re-layouts  15.4 us

profile of v1, /device:TPU:1, one launch (start us, length us, event | category | flops | bytes accessed | tf_op | source)
XLA Modules:
  0.0 90.3 jit_solution(10223421083469544686)
XLA Ops:
  0.6 0.7 stack.9
  1.3 0.7 stack.10
  2.0 0.0 copy-start
  2.0 2.2 %copy-done = bf16[16,512,2,128]{3,2,1,0:T(2,128)(2,1)S(1)} copy-done((bf16[16,512,2,128]{3,2,1,0:T(2,128)(2,1)S(1)}, bf16[16,512,2,128]{3,2,1,0:T(2,128)(2,1)}, u32[]{:S(2)}) %copy-start) | copy-done | bytes 4194328
  4.2 0.0 copy-start.1
  4.2 2.2 %copy-done.1 = bf16[16,512,2,128]{3,2,1,0:T(2,128)(2,1)S(1)} copy-done((bf16[16,512,2,128]{3,2,1,0:T(2,128)(2,1)S(1)}, bf16[16,512,2,128]{3,2,1,0:T(2,128)(2,1)}, u32[]{:S(2)}) %copy-start.1) | copy-done | bytes 4194328
  6.3 0.0 copy-start.2
  6.3 1.2 %copy-done.2 = bf16[168,2688]{1,0:T(8,128)(2,1)S(1)} copy-done((bf16[168,2688]{1,0:T(8,128)(2,1)S(1)}, bf16[168,2688]{1,0:T(8,128)(2,1)}, u32[]{:S(2)}) %copy-start.2) | copy-done | bytes 903192
  7.5 0.0 copy-start.3
  7.5 1.2 %copy-done.3 = bf16[168,2688]{1,0:T(8,128)(2,1)S(1)} copy-done((bf16[168,2688]{1,0:T(8,128)(2,1)S(1)}, bf16[168,2688]{1,0:T(8,128)(2,1)}, u32[]{:S(2)}) %copy-start.3) | copy-done | bytes 903192
  8.7 0.0 copy-start.4
  8.7 1.2 %copy-done.4 = bf16[2688,168]{0,1:T(8,128)(2,1)S(1)} copy-done((bf16[2688,168]{0,1:T(8,128)(2,1)S(1)}, bf16[2688,168]{0,1:T(8,128)(2,1)}, u32[]{:S(2)}) %copy-start.4) | copy-done | bytes 903192
  9.9 0.0 copy-start.5
  9.9 0.9 %copy-done.5 = bf16[168,512]{1,0:T(8,128)(2,1)S(1)} copy-done((bf16[168,512]{1,0:T(8,128)(2,1)S(1)}, bf16[168,512]{1,0:T(8,128)(2,1)}, u32[]{:S(2)}) %copy-start.5) | copy-done | bytes 172056
  10.8 0.9 %copy-done.6 = bf16[512,168]{0,1:T(8,128)(2,1)S(1)} copy-done((bf16[512,168]{0,1:T(8,128)(2,1)S(1)}, bf16[512,168]{0,1:T(8,128)(2,1)}, u32[]{:S(2)}) %copy-start.6) | copy-done | bytes 172056
  11.7 0.9 copy-done.7
  12.6 0.9 copy-done.8
  13.5 0.7 copy-done.9
  14.2 0.7 copy-done.10
  14.9 0.7 copy-done.11
  15.5 0.7 copy-done.12
  16.2 72.9 %shard_map.158 = (bf16[16,168]{1,0:T(8,128)(2,1)S(1)}, bf16[16,168]{1,0:T(8,128)(2,1)S(1)}) custom-call(s32[16]{0:T(128)S(1)} %copy-done.11, s32[16]{0:T(128)S(1)} %copy-done.12, bf16[16,168]{1,0:T(8,128)(2,1)S(1)} %copy-done.9, bf16[16,168]{1,0:T(8,128)(2,1)S(1)} %copy-done.10, f32[2,168]{1,0:T(2,128)S(1)} %maximum_convert_fusion.gains_hbm, ...), custom_call_target="tpu_custom_call" | custom-call | tf_op jit(solution)/shard_map/pallas_call | solution.py:410
  89.1 0.6 copy.19
  89.7 0.6 copy.20
  (8 shorter events, 0.0 us)
Async XLA Ops:
  2.0 2.2 %copy-start = (bf16[16,512,2,128]{3,2,1,0:T(2,128)(2,1)S(1)}, bf16[16,512,2,128]{3,2,1,0:T(2,128)(2,1)}, u32[]{:S(2)}) copy-start(bf16[16,512,2,128]{3,2,1,0:T(2,128)(2,1)} %param.26) | copy-start | bytes 12582916
  4.2 2.2 %copy-start.1 = (bf16[16,512,2,128]{3,2,1,0:T(2,128)(2,1)S(1)}, bf16[16,512,2,128]{3,2,1,0:T(2,128)(2,1)}, u32[]{:S(2)}) copy-start(bf16[16,512,2,128]{3,2,1,0:T(2,128)(2,1)} %param.27) | copy-start | bytes 12582916
  6.3 1.2 %copy-start.2 = (bf16[168,2688]{1,0:T(8,128)(2,1)S(1)}, bf16[168,2688]{1,0:T(8,128)(2,1)}, u32[]{:S(2)}) copy-start(bf16[168,2688]{1,0:T(8,128)(2,1)} %wg_hbm.1) | copy-start | bytes 2709508
  7.5 1.2 %copy-start.3 = (bf16[168,2688]{1,0:T(8,128)(2,1)S(1)}, bf16[168,2688]{1,0:T(8,128)(2,1)}, u32[]{:S(2)}) copy-start(bf16[168,2688]{1,0:T(8,128)(2,1)} %wu_hbm.1) | copy-start | bytes 2709508
  8.7 1.2 %copy-start.4 = (bf16[2688,168]{0,1:T(8,128)(2,1)S(1)}, bf16[2688,168]{0,1:T(8,128)(2,1)}, u32[]{:S(2)}) copy-start(bf16[2688,168]{0,1:T(8,128)(2,1)} %param.25) | copy-start | bytes 2709508
  9.9 0.9 %copy-start.5 = (bf16[168,512]{1,0:T(8,128)(2,1)S(1)}, bf16[168,512]{1,0:T(8,128)(2,1)}, u32[]{:S(2)}) copy-start(bf16[168,512]{1,0:T(8,128)(2,1)} %wq_hbm.1) | copy-start | bytes 516100
  10.8 0.9 %copy-start.6 = (bf16[512,168]{0,1:T(8,128)(2,1)S(1)}, bf16[512,168]{0,1:T(8,128)(2,1)}, u32[]{:S(2)}) copy-start(bf16[512,168]{0,1:T(8,128)(2,1)} %param.21) | copy-start | bytes 516100
  11.7 0.9 copy-start.7
  12.6 0.9 copy-start.8
  13.5 0.7 copy-start.9
  14.2 0.7 copy-start.10
  14.9 0.7 copy-start.11
  15.5 0.7 copy-start.12

commit v2 on v1

--- a/solution.py
+++ b/solution.py
@@ -25,18 +25,17 @@
 F32 = jnp.float32
 BF16 = jnp.bfloat16
 
-N_LOCAL = 15
-
 
 def iota(shape, dim):
     return lax.broadcasted_iota(jnp.int32, shape, dim)
 
 
+def ring_peer(me, i, size=8):
+    return lax.rem(me + size // 2 + ((i + 1) // 2) * (1 - 2 * (i % 2)), size)
+
+
 def peer_of(x, z, i):
-    zi, xi = i // 4, i % 4
-    zo = 4 + ((zi + 1) // 2) * (1 - 2 * (zi % 2))
-    xo = 2 + ((xi + 1) // 2) * (1 - 2 * (xi % 2))
-    return lax.rem(x + xo, 4) * 8 + lax.rem(z + zo, 8)
+    return ring_peer(x, i % 4, 4) * 8 + ring_peer(z, i // 4)
 
 
 def nt_dot(a, b):
@@ -44,11 +43,12 @@
 
 
 def kernel(
-    lengths,
-    granularity,
+    lengths_hbm,
+    granularity_hbm,
     x1_hbm,
     x2_hbm,
-    gains_hbm,
+    gain1_hbm,
+    gain2_hbm,
     wq_hbm,
     wk_hbm,
     wv_hbm,
@@ -60,9 +60,12 @@
     vc_hbm,
     o1_ref,
     o2_ref,
+    lengths,
+    granularity,
     x1,
     x2,
-    gains,
+    gain1,
+    gain2,
     wq,
     wk,
     wv,
@@ -83,13 +86,18 @@
     sq_out,
     sq_in,
     gu_out,
-    gu_in,
-    gu_in2,
+    gx_in,
+    gz_out,
+    gz_in,
+    gz_in2,
     hid_all,
     down_in,
     local_sem,
     send_sem,
     recv_sem,
+    gx_send,
+    gx_recv,
+    gz_send,
 ):
     c = lax.axis_index("context")
     t = lax.axis_index("tensor")
@@ -101,7 +109,7 @@
     loads = [
         local(0, x1_hbm, x1),
         local(1, x2_hbm, x2),
-        local(2, gains_hbm, gains),
+        local(2, gain1_hbm, gain1),
         local(3, wq_hbm, wq),
         local(4, wk_hbm, wk),
         local(5, wv_hbm, wv),
@@ -111,10 +119,10 @@
         local(9, wg_hbm, wg),
         local(10, wu_hbm, wu),
         local(11, wd_hbm, wd),
+        local(12, gain2_hbm, gain2),
+        local(13, lengths_hbm, lengths),
+        local(14, granularity_hbm, granularity),
     ]
-    for load in loads:
-        load.start()
-
     barrier = pltpu.get_barrier_semaphore()
 
     @pl.loop(0, CTX - 1)
@@ -123,11 +131,14 @@
             barrier, inc=1, device_id=(peer_of(x, z, i), t), device_id_type=MESH
         )
 
-    @pl.loop(1, TEN)
-    def _(d):
+    @pl.loop(0, TEN - 1)
+    def _(i):
         pl.semaphore_signal(
-            barrier, inc=1, device_id=(c, lax.rem(t + d, TEN)), device_id_type=MESH
+            barrier, inc=1, device_id=(c, ring_peer(t, i)), device_id_type=MESH
         )
+
+    for load in loads:
+        load.start()
 
     def send(phase, src, dst, peer):
         pltpu.make_async_remote_copy(
@@ -142,10 +153,15 @@
     def wait(sem, ref):
         pltpu.make_async_copy(ref, ref, sem).wait()
 
+    left = []
+
+    def leaves(phase, ref):
+        left.append(lambda: wait(send_sem.at[phase], ref))
+
     for i in range(6):
         loads[i].wait()
     rows = jnp.concatenate([x1[...], x2[...]], axis=0).astype(F32)
-    gated = (rows * gains[0:1, :]).astype(BF16)
+    gated = (rows * gain1[...].astype(F32)[None, :]).astype(BF16)
     q_part = jnp.dot(gated, wq[...], preferred_element_type=F32)
     k_part = jnp.dot(gated, wk[...], preferred_element_type=F32)
     v_part = jnp.dot(gated, wv[...], preferred_element_type=F32)
@@ -171,6 +187,8 @@
         p = peer_of(x, z, i)
         send(0, qkv_out.at[p], qkv_in.at[i], (p, t))
 
+    leaves(0, qkv_in.at[pl.ds(0, CTX - 1)])
+
     qkv_in[CTX - 1] = qkv_out[c]
     wait(recv_sem.at[0], qkv_in.at[pl.ds(0, CTX - 1)])
     total = jnp.sum(qkv_in[...].astype(F32), axis=0)
@@ -184,31 +202,49 @@
         tile = qkv_all.at[pl.ds(mine, 8)]
         send(1, tile, tile, (peer_of(x, z, i), t))
 
+    leaves(1, qkv_all.at[pl.ds(0, 8 * (CTX - 1))])
+
     wait(recv_sem.at[1], qkv_all.at[pl.ds(0, 8 * (CTX - 1))])
 
+    loads[13].wait()
     loads[6].wait()
     loads[7].wait()
     lane = iota((8, 2 * POS), 1)
     own_head = (lane % 2) == (iota((8, 2 * POS), 0) // 4)
     position = c * POS + lane // 2
 
-    @pl.loop(0, REQS)
-    def _(r):
-        queries = qkv_all[pl.ds(r, 8, stride=16), :].astype(BF16)
-        scores = nt_dot(queries, kc[r]) * SCALE
-        live = own_head & (position < lengths[r])
-        peak = jnp.max(jnp.where(live, scores, MASKED), axis=1, keepdims=True)
-        weights = jnp.where(live, jnp.exp(scores - peak), 0.0)
-        sums = jnp.sum(weights, axis=1, keepdims=True)
-        mixture = jnp.dot(weights.astype(BF16), vc[r], preferred_element_type=F32)
-        stats = jnp.where(iota((8, HEAD), 1) < 64, peak, sums)
-        mix_out[2 * r] = jnp.concatenate([mixture[0:4], stats[0:4]], axis=0)
-        mix_out[2 * r + 1] = jnp.concatenate([mixture[4:8], stats[4:8]], axis=0)
-
-    @pl.loop(0, CTX - 1)
-    def _(i):
-        p = peer_of(x, z, i)
-        send(2, mix_out.at[p], mix_in.at[i], (p, t))
+    @pl.loop(0, 2)
+    def _(n):
+        homes = [ring_peer(x, 2 * n + m, 4) for m in range(2)]
+        requests = [home * 4 + m for home in homes for m in range(4)]
+        queries = [qkv_all[pl.ds(r, 8, stride=16), :].astype(BF16) for r in requests]
+        scores = [nt_dot(q, kc[r]) * SCALE for q, r in zip(queries, requests)]
+        live = [own_head & (position < lengths[r]) for r in requests]
+        peaks = [
+            jnp.max(jnp.where(l, s, MASKED), axis=1, keepdims=True) for s, l in zip(scores, live)
+        ]
+        weights = [
+            jnp.where(l, jnp.exp(s - m), 0.0) for s, l, m in zip(scores, live, peaks)
+        ]
+        sums = [jnp.sum(w, axis=1, keepdims=True) for w in weights]
+        mixtures = [
+            jnp.dot(w.astype(BF16), vc[r], preferred_element_type=F32)
+            for w, r in zip(weights, requests)
+        ]
+        for r, m, total, mixture in zip(requests, peaks, sums, mixtures):
+            stats = jnp.where(iota((8, HEAD), 1) < 64, m, total)
+            mix_out[2 * r] = jnp.concatenate([mixture[0:4], stats[0:4]], axis=0)
+            mix_out[2 * r + 1] = jnp.concatenate([mixture[4:8], stats[4:8]], axis=0)
+
+        @pl.loop(0, 16)
+        def _(i):
+            p = ring_peer(x, 2 * n + i % 2, 4) * 8 + ring_peer(z, i // 2)
+
+            @pl.when(p != c)
+            def _():
+                send(2, mix_out.at[p], mix_in.at[16 * n + i], (p, t))
+
+    leaves(2, mix_in.at[pl.ds(0, CTX - 1)])
 
     mix_in[CTX - 1] = mix_out[c]
     request, kv = c // 2, c % 2
@@ -242,6 +278,8 @@
         tile = att_all.at[pl.ds(mine, 8)]
         send(3, tile, tile, (peer_of(x, z, i), t))
 
+    leaves(3, att_all.at[pl.ds(0, 8 * (CTX - 1))])
+
     loads[8].wait()
     wait(recv_sem.at[3], att_all.at[pl.ds(0, 8 * (CTX - 1))])
 
@@ -263,9 +301,11 @@
     def over_tensor(phase, value, slots):
         proj_out[phase - 4] = jnp.concatenate([value, pad], axis=1).astype(BF16)
 
-        @pl.loop(1, TEN)
-        def _(d):
-            send(phase, proj_out.at[phase - 4], slots.at[t], (c, lax.rem(t + d, TEN)))
+        @pl.loop(0, TEN - 1)
+        def _(i):
+            send(phase, proj_out.at[phase - 4], slots.at[t], (c, ring_peer(t, i)))
+
+        leaves(phase, slots.at[pl.ds(0, TEN - 1)])
 
         slots[t] = proj_out[phase - 4]
         wait(recv_sem.at[phase], slots.at[pl.ds(0, TEN - 1)])
@@ -277,42 +317,120 @@
     diagonal = iota((ROWS, HEAD), 0) == iota((ROWS, HEAD), 1)
     sq_out[...] = jnp.sum(jnp.where(diagonal, square, 0.0), axis=0, keepdims=True)
 
+    sq_in[CTX - 1] = sq_out[...]
+    loads[12].wait()
+    loads[14].wait()
+    ffn_gated = (residual * gain2[...].astype(F32)[None, :]).astype(BF16)
+    loads[9].wait()
+    loads[10].wait()
+
+    def partial(k, tiles):
+        columns = pl.ds(pl.multiple_of(k * 256, 256), HEAD * tiles)
+        gate = jnp.dot(ffn_gated, wg[:, columns], preferred_element_type=F32).astype(BF16)
+        up = jnp.dot(ffn_gated, wu[:, columns], preferred_element_type=F32).astype(BF16)
+        for a in range(2 * tiles):
+            rows_of, columns_of = slice(a % 2 * 16, a % 2 * 16 + 16), slice(a // 2 * HEAD, a // 2 * HEAD + HEAD)
+            gu_out[4 * k + a, 0:16, :] = gate[rows_of, columns_of]
+            gu_out[4 * k + a, 16:32, :] = up[rows_of, columns_of]
+
+    def along_x(n, k, i):
+        a = ring_peer(x, i, 4)
+        pltpu.make_async_remote_copy(
+            src_ref=gu_out.at[4 * k + a],
+            dst_ref=gx_in.at[n, i],
+            send_sem=gx_send.at[n],
+            recv_sem=gx_recv.at[n],
+            device_id=(a * 8 + z, t),
+            device_id_type=MESH,
+        ).start()
+
+    for n in range(3):
+        partial(8 + n, 2 if n < 2 else 1)
+        for i in range(3):
+            if n < 2:
+                along_x(n, 8 + n, i)
+            else:
+
+                @pl.when(ring_peer(x, i, 4) < 2)
+                def _():
+                    along_x(2, 10, i)
+
+    @pl.loop(0, 8)
+    def _(n):
+        k = ring_peer(z, n)
+        partial(k, 2)
+        for i in range(3):
+            along_x(3 + n, k, i)
+
     @pl.loop(0, CTX - 1)
     def _(i):
         send(6, sq_out, sq_in.at[i], (peer_of(x, z, i), t))
 
-    sq_in[CTX - 1] = sq_out[...]
-    ffn_gated = (residual * gains[1:2, :]).astype(BF16)
-    loads[9].wait()
-    loads[10].wait()
+    leaves(6, sq_in.at[pl.ds(0, CTX - 1)])
+
+    def x_sum(n, k):
+        wait(gx_recv.at[n], gx_in.at[n])
+        total = gu_out[4 * k + x].astype(F32)
+        for i in range(3):
+            total = total + gx_in[n, i].astype(F32)
+        return total.astype(BF16)
+
+    for n in range(3):
+        here = (x < 4) if n < 2 else (x < 2)
+
+        @pl.when(here & (z == n))
+        def _():
+            gz_in2[z] = x_sum(n, 8 + n)
+
+        @pl.when(here & (z != n))
+        def _():
+            gz_out[n] = x_sum(n, 8 + n)
+            pltpu.make_async_remote_copy(
+                src_ref=gz_out.at[n],
+                dst_ref=gz_in2.at[z],
+                send_sem=gz_send.at[n],
+                recv_sem=recv_sem.at[8],
+                device_id=(x * 8 + n, t),
+                device_id_type=MESH,
+            ).start()
 
     @pl.loop(0, 7)
     def _(n):
-        columns = pl.ds(pl.multiple_of(n * 384, 384), 384)
-        gate = jnp.dot(ffn_gated, wg[:, columns], preferred_element_type=F32).astype(BF16)
-        up = jnp.dot(ffn_gated, wu[:, columns], preferred_element_type=F32).astype(BF16)
-        for k in range(3):
-            for s in range(2):
-                unit = 6 * n + 2 * k + s
-                gu_out[unit, 0:16, :] = gate[s * 16 : s * 16 + 16, k * HEAD : (k + 1) * HEAD]
-                gu_out[unit, 16:32, :] = up[s * 16 : s * 16 + 16, k * HEAD : (k + 1) * HEAD]
-
-    @pl.loop(0, CTX - 1)
-    def _(i):
-        p = peer_of(x, z, i)
-        send(7, gu_out.at[p], gu_in.at[i], (p, t))
-
-    @pl.loop(0, EXTRA)
-    def _(p):
-        @pl.when(p != c)
-        def _():
-            send(8, gu_out.at[CTX + p], gu_in2.at[c], (p, t))
-
-    gu_in[CTX - 1] = gu_out[c]
+        k = ring_peer(z, n)
+        gz_out[3 + n] = x_sum(3 + n, k)
+        send(7, gz_out.at[3 + n], gz_in.at[n], (x * 8 + k, t))
+
+    gz_in[7] = x_sum(10, z)
+    leaves(7, gz_in.at[pl.ds(0, 7)])
+
+    def sent_extra():
+        for n in range(3):
+            if n < 2:
+                wait(gx_send.at[n], gx_in.at[n])
+            else:
+
+                @pl.when(x < 2)
+                def _():
+                    wait(gx_send.at[n], gx_in.at[n, pl.ds(0, 1)])
+
+                @pl.when(x >= 2)
+                def _():
+                    wait(gx_send.at[n], gx_in.at[n, pl.ds(0, 2)])
+
+            @pl.when(((x < 4) if n < 2 else (x < 2)) & (z != n))
+            def _():
+                wait(gz_send.at[n], gz_out.at[n])
+
+        @pl.loop(3, 11)
+        def _(n):
+            wait(gx_send.at[n], gx_in.at[n])
+
+    left.append(sent_extra)
+    extra = (z < 2) | ((z == 2) & (x < 2))
 
     wait(recv_sem.at[6], sq_in.at[pl.ds(0, CTX - 1)])
     squares = jnp.sum(sq_in[...], axis=0)
-    step_rows = iota((REQS, HEAD), 1) == iota((REQS, HEAD), 0) + REQS * (c % 2)
+    step_rows = iota((REQS, HEAD), 1) == iota((REQS, HEAD), 0) + REQS * (x % 2)
     squares = jnp.sum(jnp.where(step_rows, squares, 0.0), axis=1, keepdims=True)
     ffn_inv = lax.rsqrt(squares / WIDTH + EPS)
     levels = jnp.zeros((REQS, 1), jnp.int32)
@@ -334,28 +452,38 @@
         def _(i):
             send(phase, part_of, part_of, (peer_of(x, z, i), t))
 
-    wait(recv_sem.at[7], gu_in.at[pl.ds(0, CTX - 1)])
-    hid_all[pl.ds(pl.multiple_of(c * 16, 16), 16), :] = hidden_of(gu_in)
-    share(9, c)
-
-    @pl.when(c < EXTRA)
+    def unit_rows(unit):
+        return pl.ds(pl.multiple_of(unit * 16, 16), 16)
+
+    @pl.when(extra)
     def _():
-        gu_in2[c] = gu_out[CTX + c]
-        wait(recv_sem.at[8], gu_in2.at[pl.ds(0, CTX - 1)])
-        hid_all[pl.ds(pl.multiple_of((CTX + c) * 16, 16), 16), :] = hidden_of(gu_in2)
-        share(10, CTX + c)
+        wait(recv_sem.at[8], gz_in2.at[pl.ds(0, 7)])
+        hid_all[unit_rows(32 + 4 * z + x), :] = hidden_of(gz_in2)
+        share(10, 32 + 4 * z + x)
+
+    wait(recv_sem.at[7], gz_in.at[pl.ds(0, 7)])
+    hid_all[unit_rows(4 * z + x), :] = hidden_of(gz_in)
+    share(9, 4 * z + x)
+    leaves(9, hid_all.at[pl.ds(0, 16 * (CTX - 1))])
+
+    def second_left():
+        @pl.when(extra)
+        def _():
+            wait(send_sem.at[10], hid_all.at[pl.ds(0, 16 * (CTX - 1))])
+
+    left.append(second_left)
 
     loads[11].wait()
-    wait(recv_sem.at[9], hid_all.at[pl.ds(0, 16 * (CTX - 1))])
-
-    @pl.when(c < EXTRA)
+
+    @pl.when(extra)
     def _():
         wait(recv_sem.at[10], hid_all.at[pl.ds(0, 16 * (EXTRA - 1))])
 
-    @pl.when(c >= EXTRA)
+    @pl.when(jnp.logical_not(extra))
     def _():
         wait(recv_sem.at[10], hid_all.at[pl.ds(0, 16 * EXTRA)])
 
+    wait(recv_sem.at[9], hid_all.at[pl.ds(0, 16 * (CTX - 1))])
     hidden = jnp.concatenate(
         [hid_all[i * ROWS : (i + 1) * ROWS, :] for i in range(TILES)], axis=1
     )
@@ -364,25 +492,8 @@
     o1_ref[...] = output[0:REQS]
     o2_ref[...] = output[REQS:ROWS]
 
-    wait(send_sem.at[0], qkv_in.at[pl.ds(0, CTX - 1)])
-    wait(send_sem.at[1], qkv_all.at[pl.ds(0, 8 * (CTX - 1))])
-    wait(send_sem.at[2], mix_in.at[pl.ds(0, CTX - 1)])
-    wait(send_sem.at[3], att_all.at[pl.ds(0, 8 * (CTX - 1))])
-    wait(send_sem.at[4], proj_in.at[pl.ds(0, TEN - 1)])
-    wait(send_sem.at[5], down_in.at[pl.ds(0, TEN - 1)])
-    wait(send_sem.at[6], sq_in.at[pl.ds(0, CTX - 1)])
-    wait(send_sem.at[7], gu_in.at[pl.ds(0, CTX - 1)])
-
-    wait(send_sem.at[9], hid_all.at[pl.ds(0, 16 * (CTX - 1))])
-
-    @pl.when(c < EXTRA)
-    def _():
-        wait(send_sem.at[8], gu_in.at[pl.ds(0, EXTRA - 1)])
-        wait(send_sem.at[10], hid_all.at[pl.ds(0, 16 * (CTX - 1))])
-
-    @pl.when(c >= EXTRA)
-    def _():
-        wait(send_sem.at[8], gu_in.at[pl.ds(0, EXTRA)])
+    for sent in left:
+        sent()
 
 
 def per_device(
@@ -402,9 +513,7 @@
     lengths,
     granularity,
 ):
-    gains = jnp.stack([attn_gain, ffn_gain]).astype(F32)
-    any_space = pl.BlockSpec(memory_space=pl.ANY)
-    smem = pl.BlockSpec(memory_space=pltpu.SMEM)
+    hbm = pl.BlockSpec(memory_space=pltpu.HBM)
     vmem = pl.BlockSpec(memory_space=pltpu.VMEM)
     V = pltpu.VMEM
     return pl.pallas_call(
@@ -413,12 +522,15 @@
             jax.ShapeDtypeStruct((REQS, COLS), BF16),
             jax.ShapeDtypeStruct((REQS, COLS), BF16),
         ),
-        in_specs=[smem, smem] + [any_space] * 12,
+        in_specs=[hbm] * 15,
         out_specs=(vmem, vmem),
         scratch_shapes=[
+            pltpu.SMEM((REQS,), jnp.int32),
+            pltpu.SMEM((REQS,), jnp.int32),
             V((REQS, COLS), BF16),
             V((REQS, COLS), BF16),
-            V((2, COLS), F32),
+            V((COLS,), BF16),
+            V((COLS,), BF16),
             V((COLS, 512), BF16),
             V((COLS, 256), BF16),
             V((COLS, 256), BF16),
@@ -439,23 +551,29 @@
             V((1, HEAD), F32),
             V((CTX, 1, HEAD), F32),
             V((2 * TILES, 32, HEAD), BF16),
-            V((CTX, 32, HEAD), BF16),
-            V((CTX, 32, HEAD), BF16),
+            V((11, 3, 32, HEAD), BF16),
+            V((10, 32, HEAD), BF16),
+            V((8, 32, HEAD), BF16),
+            V((8, 32, HEAD), BF16),
             V((TILES * ROWS, HEAD), BF16),
             V((TEN, ROWS, 2 * HEAD), BF16),
-            pltpu.SemaphoreType.DMA((12,)),
+            pltpu.SemaphoreType.DMA((15,)),
             pltpu.SemaphoreType.DMA((11,)),
             pltpu.SemaphoreType.DMA((11,)),
+            pltpu.SemaphoreType.DMA((11,)),
+            pltpu.SemaphoreType.DMA((11,)),
+            pltpu.SemaphoreType.DMA((3,)),
         ],
         compiler_params=pltpu.CompilerParams(
-            collective_id=0, has_side_effects=True, vmem_limit_bytes=40 * 2**20
+            collective_id=0, has_side_effects=True, vmem_limit_bytes=56 * 2**20
         ),
     )(
         lengths,
         granularity,
         first_input,
         second_input,
-        gains,
+        attn_gain,
+        ffn_gain,
         query_weight,
         key_weight,
         value_weight,

time: 90.8 us -> 67.1 us (0.74)
  local copies, waits for them, and re-layouts: 16.7 us -> 2.59 us
  Pallas kernels: 72.9 us -> 63.5 us
    unnamed x28 -> x2, local copies, waits for them, and re-layouts: 15.4 us -> 2.59 us
    pallas_call x1, Pallas kernels: 72.9 us -> 63.5 us  [per_device(): pl.pallas_call(kernel, out_shape=(jax.ShapeDtypeStruct((REQS, COLS), BF16...]
    another operation x2 -> x0, local copies, waits for them, and re-layouts: 1.32 us -> none  [per_device(): gains = jnp.stack([attn_gain, ffn_gain]).astype(F32)]
where the time goes in v2:
time: 67.1 us; the launch traced here: 66.8 us
  Pallas kernels  63.5 us (95%)
  local copies, waits for them, and re-layouts  2.59 us (4%)
    pallas_call x1, Pallas kernels, per_device(): pl.pallas_call(kernel, out_shape=(jax.ShapeDtypeStruct((REQS, COLS), BF16...  63.5 us
    unnamed x2, local copies, waits for them, and re-layouts  2.59 us

profile of v2, /device:TPU:1, one launch (start us, length us, event | category | flops | bytes accessed | tf_op | source)
XLA Modules:
  0.0 66.8 jit_solution(3574436120890705816)
XLA Ops:
  0.6 63.5 %shard_map.158 = (bf16[16,168]{1,0:T(8,128)(2,1)}, bf16[16,168]{1,0:T(8,128)(2,1)}) custom-call(s32[16]{0:T(128)} %lengths_hbm.1, s32[16]{0:T(128)} %granularity_hbm.1, bf16[16,168]{1,0:T(8,128)(2,1)} %x1_hbm.1, bf16[16,168]{1,0:T(8,128)(2,1)} %x2_hbm.1, bf16[168]{0:T(256)(128)(2,1)} %gain1_hbm.1, bf16[168]{0:T(256)(128)(2,1)} %gain2_hbm.1, ...), custom_call_target="tpu_custom_call" | custom-call | tf_op jit(solution)/shard_map/pallas_call | solution.py:519
  64.2 1.3 %copy.19 = bf16[16,168]{1,0:T(8,128)(2,1)} copy(bf16[16,168]{1,0:T(8,128)(2,1)} %get-tuple-element.4) | data formatting | bytes 10752
  65.5 1.3 %copy.20 = bf16[16,168]{1,0:T(8,128)(2,1)} copy(bf16[16,168]{1,0:T(8,128)(2,1)} %get-tuple-element.5) | data formatting | bytes 10752

commit v3 on v2

--- a/solution.py
+++ b/solution.py
@@ -75,8 +75,15 @@
     wd,
     kc,
     vc,
-    qkv_out,
-    qkv_in,
+    q_out,
+    qx_in,
+    qz_in,
+    kv_out,
+    kvx_in,
+    kvz_in,
+    new_sq,
+    sqx_in,
+    sqz_in,
     qkv_all,
     mix_out,
     mix_in,
@@ -125,10 +132,16 @@
     ]
     barrier = pltpu.get_barrier_semaphore()
 
-    @pl.loop(0, CTX - 1)
+    @pl.loop(0, 7)
     def _(i):
         pl.semaphore_signal(
-            barrier, inc=1, device_id=(peer_of(x, z, i), t), device_id_type=MESH
+            barrier, inc=1, device_id=(x * 8 + ring_peer(z, i), t), device_id_type=MESH
+        )
+
+    @pl.loop(0, 3)
+    def _(i):
+        pl.semaphore_signal(
+            barrier, inc=1, device_id=(ring_peer(x, i, 4) * 8 + z, t), device_id_type=MESH
         )
 
     @pl.loop(0, TEN - 1)
@@ -165,46 +178,62 @@
     q_part = jnp.dot(gated, wq[...], preferred_element_type=F32)
     k_part = jnp.dot(gated, wk[...], preferred_element_type=F32)
     v_part = jnp.dot(gated, wv[...], preferred_element_type=F32)
-    part = jnp.concatenate([q_part, k_part, v_part], axis=1)
-    square = jnp.sum(rows * rows, axis=1, keepdims=True)
-    square_hi = square.astype(BF16).astype(F32)
-    square_tile = jnp.where(iota((ROWS, HEAD), 1) == 0, square_hi, square - square_hi)
-    for j in range(8):
-        for g in range(4):
-            tile = jnp.concatenate(
-                [
-                    part[g * 8 : g * 8 + 8, j * HEAD : (j + 1) * HEAD],
-                    square_tile[g * 8 : g * 8 + 8, :],
-                ],
-                axis=0,
-            )
-            qkv_out[j * 4 + g] = tile.astype(BF16)
-
-    pl.semaphore_wait(barrier, CTX - 1 + TEN - 1)
-
-    @pl.loop(0, CTX - 1)
-    def _(i):
-        p = peer_of(x, z, i)
-        send(0, qkv_out.at[p], qkv_in.at[i], (p, t))
-
-    leaves(0, qkv_in.at[pl.ds(0, CTX - 1)])
-
-    qkv_in[CTX - 1] = qkv_out[c]
-    wait(recv_sem.at[0], qkv_in.at[pl.ds(0, CTX - 1)])
-    total = jnp.sum(qkv_in[...].astype(F32), axis=0)
-    squares = total[8:16, 0:1] + total[8:16, 1:2]
+    q_out[0] = q_part[0:REQS].astype(BF16)
+    q_out[1] = q_part[REQS:ROWS].astype(BF16)
+    kv_out[0] = jnp.concatenate([k_part, v_part], axis=1).astype(BF16)
+    diagonal = iota((ROWS, HEAD), 0) == iota((ROWS, HEAD), 1)
+
+    def as_row(column):
+        return jnp.sum(jnp.where(diagonal, column, 0.0), axis=0, keepdims=True)
+
+    def as_column(row):
+        return jnp.sum(jnp.where(diagonal, row, 0.0), axis=1, keepdims=True)
+
+    new_sq[0] = as_row(jnp.sum(rows * rows, axis=1, keepdims=True))
+
+    pl.semaphore_wait(barrier, 7 + 3 + TEN - 1)
+
+    def along_x_all(phase, src, slots):
+        @pl.loop(0, 3)
+        def _(i):
+            send(phase, src, slots.at[i], (ring_peer(x, i, 4) * 8 + z, t))
+
+        leaves(phase, slots)
+
+    def along_z_all(phase, src, slots):
+        @pl.loop(0, 7)
+        def _(i):
+            send(phase, src, slots.at[i], (x * 8 + ring_peer(z, i), t))
+
+        leaves(phase, slots)
+
+    def sum_of(phase, own, slots):
+        wait(recv_sem.at[phase], slots)
+        return own[...].astype(F32) + jnp.sum(slots[...].astype(F32), axis=0)
+
+    along_z_all(1, q_out.at[1], qz_in.at[1])
+    along_x_all(0, q_out.at[0], qx_in.at[0])
+    along_x_all(11, new_sq.at[0], sqx_in)
+    along_x_all(12, kv_out.at[0], kvx_in)
+    new_sq[1] = sum_of(11, new_sq.at[0], sqx_in)
+    q_out[2] = sum_of(0, q_out.at[0], qx_in.at[0]).astype(BF16)
+    along_z_all(13, q_out.at[2], qz_in.at[0])
+    along_z_all(14, new_sq.at[1], sqz_in)
+    q_out[3] = sum_of(1, q_out.at[1], qz_in.at[1]).astype(BF16)
+    along_x_all(15, q_out.at[3], qx_in.at[1])
+    kv_out[1] = sum_of(12, kv_out.at[0], kvx_in).astype(BF16)
+    along_z_all(16, kv_out.at[1], kvz_in)
+    squares = as_column(sum_of(14, new_sq.at[1], sqz_in))
     inv = lax.rsqrt(squares / WIDTH + EPS)
-    mine = pl.multiple_of(c * 8, 8)
-    qkv_all[pl.ds(mine, 8), :] = (total[0:8, :] * inv).astype(BF16).astype(F32)
-
-    @pl.loop(0, CTX - 1)
-    def _(i):
-        tile = qkv_all.at[pl.ds(mine, 8)]
-        send(1, tile, tile, (peer_of(x, z, i), t))
-
-    leaves(1, qkv_all.at[pl.ds(0, 8 * (CTX - 1))])
-
-    wait(recv_sem.at[1], qkv_all.at[pl.ds(0, 8 * (CTX - 1))])
+    totals = [
+        sum_of(13, q_out.at[2], qz_in.at[0]),
+        sum_of(15, q_out.at[3], qx_in.at[1]),
+    ]
+    for s in range(2):
+        query = (totals[s] * inv[s * REQS : s * REQS + REQS]).astype(BF16).astype(F32)
+        for j in range(4):
+            start = (2 * j + s) * REQS
+            qkv_all[start : start + REQS, :] = query[:, j * HEAD : (j + 1) * HEAD]
 
     loads[13].wait()
     loads[6].wait()
@@ -248,6 +277,10 @@
 
     mix_in[CTX - 1] = mix_out[c]
     request, kv = c // 2, c % 2
+    mine = pl.multiple_of(c * 8, 8)
+    new = (sum_of(16, kv_out.at[1], kvz_in) * inv).astype(BF16).astype(F32)
+    for j in range(4):
+        qkv_all[(4 + j) * ROWS : (5 + j) * ROWS, :] = new[:, j * HEAD : (j + 1) * HEAD]
 
     def new_row(j, s):
         return qkv_all[pl.ds(j * 32 + s * 16 + request, 1), :]
@@ -314,8 +347,7 @@
     residual = rows + over_tensor(4, nt_dot(att, wo[...]), proj_in)
 
     square = jnp.sum(residual * residual, axis=1, keepdims=True)
-    diagonal = iota((ROWS, HEAD), 0) == iota((ROWS, HEAD), 1)
-    sq_out[...] = jnp.sum(jnp.where(diagonal, square, 0.0), axis=0, keepdims=True)
+    sq_out[...] = as_row(square)
 
     sq_in[CTX - 1] = sq_out[...]
     loads[12].wait()
@@ -519,8 +551,8 @@
     return pl.pallas_call(
         kernel,
         out_shape=(
-            jax.ShapeDtypeStruct((REQS, COLS), BF16),
-            jax.ShapeDtypeStruct((REQS, COLS), BF16),
+            pltpu.VMEM((REQS, COLS), BF16),
+            pltpu.VMEM((REQS, COLS), BF16),
         ),
         in_specs=[hbm] * 15,
         out_specs=(vmem, vmem),
@@ -540,8 +572,15 @@
             V((COLS, 2688), BF16),
             V((REQS, 2 * POS, HEAD), BF16),
             V((REQS, 2 * POS, HEAD), BF16),
-            V((CTX, 16, HEAD), BF16),
-            V((CTX, 16, HEAD), BF16),
+            V((4, REQS, 512), BF16),
+            V((2, 3, REQS, 512), BF16),
+            V((2, 7, REQS, 512), BF16),
+            V((2, ROWS, 512), BF16),
+            V((3, ROWS, 512), BF16),
+            V((7, ROWS, 512), BF16),
+            V((2, 1, HEAD), F32),
+            V((3, 1, HEAD), F32),
+            V((7, 1, HEAD), F32),
             V((CTX * 8, HEAD), F32),
             V((CTX, 8, HEAD), F32),
             V((CTX, 8, HEAD), F32),
@@ -558,8 +597,8 @@
             V((TILES * ROWS, HEAD), BF16),
             V((TEN, ROWS, 2 * HEAD), BF16),
             pltpu.SemaphoreType.DMA((15,)),
-            pltpu.SemaphoreType.DMA((11,)),
-            pltpu.SemaphoreType.DMA((11,)),
+            pltpu.SemaphoreType.DMA((17,)),
+            pltpu.SemaphoreType.DMA((17,)),
             pltpu.SemaphoreType.DMA((11,)),
             pltpu.SemaphoreType.DMA((11,)),
             pltpu.SemaphoreType.DMA((3,)),

time: 67.1 us -> 62.7 us (0.934)
  Pallas kernels: 63.5 us -> 60.7 us
  local copies, waits for them, and re-layouts: 2.59 us -> 1.2 us
    pallas_call x1, Pallas kernels: 63.5 us -> 60.7 us  [per_device(): pl.pallas_call(kernel, out_shape=(pltpu.VMEM((REQS, COLS), BF16), pltpu.V...]
    unnamed x2, local copies, waits for them, and re-layouts: 2.59 us -> 1.2 us
where the time goes in v3:
time: 62.7 us; the launch traced here: 62.6 us
  Pallas kernels  60.7 us (97%)
  local copies, waits for them, and re-layouts  1.2 us (2%)
  between operations  0.64 us (1%)
    pallas_call x1, Pallas kernels, per_device(): pl.pallas_call(kernel, out_shape=(pltpu.VMEM((REQS, COLS), BF16), pltpu.V...  60.7 us

profile of v3, /device:TPU:1, one launch (start us, length us, event | category | flops | bytes accessed | tf_op | source)
XLA Modules:
  0.0 62.6 jit_solution(12378738904977590004)
XLA Ops:
  0.6 60.7 %shard_map.158 = (bf16[16,168]{1,0:T(8,128)(2,1)S(1)}, bf16[16,168]{1,0:T(8,128)(2,1)S(1)}) custom-call(s32[16]{0:T(128)} %lengths_hbm.1, s32[16]{0:T(128)} %granularity_hbm.1, bf16[16,168]{1,0:T(8,128)(2,1)} %x1_hbm.1, bf16[16,168]{1,0:T(8,128)(2,1)} %x2_hbm.1, bf16[168]{0:T(256)(128)(2,1)} %gain1_hbm.1, bf16[168]{0:T(256)(128)(2,1)} %gain2_hbm.1, ...), custom_call_target="tpu_custom_call" | custom-call | tf_op jit(solution)/shard_map/pallas_call | solution.py:551
  61.4 0.6 copy.19
  62.0 0.6 copy.20

commit v4 on v3

--- a/solution.py
+++ b/solution.py
@@ -38,6 +38,38 @@
     return ring_peer(x, i % 4, 4) * 8 + ring_peer(z, i // 4)
 
 
+NEAR = [
+    (0, 0),
+    (0, 1),
+    (0, 7),
+    (1, 0),
+    (3, 0),
+    (2, 0),
+    (0, 2),
+    (0, 6),
+    (1, 1),
+    (1, 7),
+    (3, 1),
+    (3, 7),
+    (0, 3),
+    (0, 5),
+    (1, 2),
+    (1, 6),
+]
+
+
+def hops(offset):
+    return min(offset[0], 4 - offset[0]) + min(offset[1], 8 - offset[1])
+
+
+def opposite(offset):
+    return ((offset[0] + 2) % 4, (offset[1] + 4) % 8)
+
+
+def far_first(offsets):
+    return sorted(offsets, key=hops, reverse=True)
+
+
 def nt_dot(a, b):
     return lax.dot_general(a, b, (((1,), (1,)), ((), ())), preferred_element_type=F32)
 
@@ -58,8 +90,7 @@
     wd_hbm,
     kc_hbm,
     vc_hbm,
-    o1_ref,
-    o2_ref,
+    out_ref,
     lengths,
     granularity,
     x1,
@@ -79,8 +110,8 @@
     qx_in,
     qz_in,
     kv_out,
-    kvx_in,
-    kvz_in,
+    kv_in,
+    inv_rows,
     new_sq,
     sqx_in,
     sqz_in,
@@ -91,7 +122,8 @@
     proj_out,
     proj_in,
     sq_out,
-    sq_in,
+    sqfx_in,
+    sqfz_in,
     gu_out,
     gx_in,
     gz_out,
@@ -144,13 +176,16 @@
             barrier, inc=1, device_id=(ring_peer(x, i, 4) * 8 + z, t), device_id_type=MESH
         )
 
+    for load in loads[0:6]:
+        load.start()
+
     @pl.loop(0, TEN - 1)
     def _(i):
         pl.semaphore_signal(
             barrier, inc=1, device_id=(c, ring_peer(t, i)), device_id_type=MESH
         )
 
-    for load in loads:
+    for load in loads[6:]:
         load.start()
 
     def send(phase, src, dst, peer):
@@ -180,7 +215,6 @@
     v_part = jnp.dot(gated, wv[...], preferred_element_type=F32)
     q_out[0] = q_part[0:REQS].astype(BF16)
     q_out[1] = q_part[REQS:ROWS].astype(BF16)
-    kv_out[0] = jnp.concatenate([k_part, v_part], axis=1).astype(BF16)
     diagonal = iota((ROWS, HEAD), 0) == iota((ROWS, HEAD), 1)
 
     def as_row(column):
@@ -214,21 +248,39 @@
     along_z_all(1, q_out.at[1], qz_in.at[1])
     along_x_all(0, q_out.at[0], qx_in.at[0])
     along_x_all(11, new_sq.at[0], sqx_in)
-    along_x_all(12, kv_out.at[0], kvx_in)
+    kv_part = jnp.concatenate([k_part, v_part], axis=1)
+    for s in range(2):
+        for j in range(4):
+            kv_out[pl.ds(4 * s + j, REQS, stride=8), :] = kv_part[
+                s * REQS : s * REQS + REQS, j * HEAD : (j + 1) * HEAD
+            ]
     new_sq[1] = sum_of(11, new_sq.at[0], sqx_in)
     q_out[2] = sum_of(0, q_out.at[0], qx_in.at[0]).astype(BF16)
     along_z_all(13, q_out.at[2], qz_in.at[0])
     along_z_all(14, new_sq.at[1], sqz_in)
     q_out[3] = sum_of(1, q_out.at[1], qz_in.at[1]).astype(BF16)
     along_x_all(15, q_out.at[3], qx_in.at[1])
-    kv_out[1] = sum_of(12, kv_out.at[0], kvx_in).astype(BF16)
-    along_z_all(16, kv_out.at[1], kvz_in)
     squares = as_column(sum_of(14, new_sq.at[1], sqz_in))
     inv = lax.rsqrt(squares / WIDTH + EPS)
-    totals = [
-        sum_of(13, q_out.at[2], qz_in.at[0]),
-        sum_of(15, q_out.at[3], qx_in.at[1]),
-    ]
+    inv_rows[...] = jnp.broadcast_to(inv, (ROWS, HEAD))
+    second_total = sum_of(15, q_out.at[3], qx_in.at[1])
+
+    def place(offset):
+        return lax.rem(x + offset[0], 4), lax.rem(z + offset[1], 8)
+
+    def request_at(at):
+        return (at[0] % 2) * 8 + lax.rem(at[1] + 4 * (at[0] // 2), 8)
+
+    def request_rows(ref, r):
+        return ref.at[pl.ds(pl.multiple_of(r * 8, 8), 8)]
+
+    for offset in far_first(NEAR + [opposite(offset) for offset in NEAR]):
+        if offset != (0, 0):
+            a, b = place(offset)
+            send(12, request_rows(kv_out, request_at((a, b))), kv_in.at[c], (a * 8 + b, t))
+
+    leaves(12, kv_in.at[pl.ds(0, CTX - 1)])
+    totals = [sum_of(13, q_out.at[2], qz_in.at[0]), second_total]
     for s in range(2):
         query = (totals[s] * inv[s * REQS : s * REQS + REQS]).astype(BF16).astype(F32)
         for j in range(4):
@@ -242,10 +294,9 @@
     own_head = (lane % 2) == (iota((8, 2 * POS), 0) // 4)
     position = c * POS + lane // 2
 
-    @pl.loop(0, 2)
-    def _(n):
-        homes = [ring_peer(x, 2 * n + m, 4) for m in range(2)]
-        requests = [home * 4 + m for home in homes for m in range(4)]
+    lane = iota((8, HEAD), 1)
+    for half in (NEAR[:8], NEAR[8:]):
+        requests = [request_at(place(offset)) for offset in half]
         queries = [qkv_all[pl.ds(r, 8, stride=16), :].astype(BF16) for r in requests]
         scores = [nt_dot(q, kc[r]) * SCALE for q, r in zip(queries, requests)]
         live = [own_head & (position < lengths[r]) for r in requests]
@@ -261,66 +312,72 @@
             for w, r in zip(weights, requests)
         ]
         for r, m, total, mixture in zip(requests, peaks, sums, mixtures):
-            stats = jnp.where(iota((8, HEAD), 1) < 64, m, total)
-            mix_out[2 * r] = jnp.concatenate([mixture[0:4], stats[0:4]], axis=0)
-            mix_out[2 * r + 1] = jnp.concatenate([mixture[4:8], stats[4:8]], axis=0)
-
-        @pl.loop(0, 16)
-        def _(i):
-            p = ring_peer(x, 2 * n + i % 2, 4) * 8 + ring_peer(z, i // 2)
-
-            @pl.when(p != c)
-            def _():
-                send(2, mix_out.at[p], mix_in.at[16 * n + i], (p, t))
+            first = m.astype(BF16).astype(F32)
+            second = (m - first).astype(BF16).astype(F32)
+            total_first = total.astype(BF16).astype(F32)
+            stats = jnp.where(lane == 3, total_first, total - total_first)
+            stats = jnp.where(lane == 2, m - first - second, stats)
+            stats = jnp.where(lane == 1, second, stats)
+            stats = jnp.where(lane == 0, first, stats)
+            stats = jnp.where(lane > 4, 0.0, stats)
+            mix_out[r] = jnp.concatenate([mixture, stats], axis=0).astype(BF16)
+        for offset in far_first(half + [opposite(offset) for offset in half]):
+            if offset != (0, 0):
+                a, b = place(offset)
+                send(2, mix_out.at[request_at((a, b))], mix_in.at[c], (a * 8 + b, t))
 
     leaves(2, mix_in.at[pl.ds(0, CTX - 1)])
 
-    mix_in[CTX - 1] = mix_out[c]
-    request, kv = c // 2, c % 2
-    mine = pl.multiple_of(c * 8, 8)
-    new = (sum_of(16, kv_out.at[1], kvz_in) * inv).astype(BF16).astype(F32)
-    for j in range(4):
-        qkv_all[(4 + j) * ROWS : (5 + j) * ROWS, :] = new[:, j * HEAD : (j + 1) * HEAD]
-
-    def new_row(j, s):
-        return qkv_all[pl.ds(j * 32 + s * 16 + request, 1), :]
-
-    query = jnp.concatenate([new_row(2 * kv + m // 2, m % 2) for m in range(4)], axis=0)
-    own = [
-        jnp.sum(query * new_row(4 + kv, s), axis=1, keepdims=True) * SCALE for s in range(2)
-    ]
-    second = (iota((4, 1), 0) % 2) == 1
-    own[1] = jnp.where(second, own[1], MASKED)
+    request = request_at((x, z))
+    mix_in[c] = mix_out[request]
+    kv_in[c] = request_rows(kv_out, request)[...]
+    query = qkv_all[pl.ds(request, 8, stride=16), :]
+    first_head = iota((8, 1), 0) < 4
+    second_step = (iota((8, 1), 0) % 2) == 1
+    inv_step = [inv_rows[pl.ds(s * REQS + request, 1), :] for s in range(2)]
+    wait(recv_sem.at[12], kv_in.at[pl.ds(0, CTX - 1)])
+    new = jnp.sum(kv_in[...], axis=0) * jnp.where(first_head, inv_step[0], inv_step[1])
+    new = new.astype(BF16).astype(F32)
+
+    def new_rows(j, s):
+        return jnp.where(first_head, new[4 * s + j : 4 * s + j + 1], new[4 * s + j + 1 : 4 * s + j + 2])
+
+    own = [jnp.sum(query * new_rows(0, s), axis=1, keepdims=True) * SCALE for s in range(2)]
+    own[1] = jnp.where(second_step, own[1], MASKED)
+    new_values = [new_rows(2, s) for s in range(2)]
     wait(recv_sem.at[2], mix_in.at[pl.ds(0, CTX - 1)])
-    mixed = mix_in[:, 0:4, :]
-    peaks = mix_in[:, 4:8, 0:1]
-    sums = mix_in[:, 4:8, 64:65]
+    mixed = mix_in[:, 0:8, :].astype(F32)
+    stats = mix_in[:, 8:16, :].astype(F32)
+    lane = iota((CTX, 8, HEAD), 2)
+    peaks = jnp.sum(jnp.where(lane < 3, stats, 0.0), axis=2, keepdims=True)
+    sums = jnp.sum(jnp.where(lane < 3, 0.0, stats), axis=2, keepdims=True)
     highest = jnp.maximum(jnp.max(peaks, axis=0), jnp.maximum(own[0], own[1]))
     rescale = jnp.exp(peaks - highest[None])
     denominator = jnp.sum(rescale * sums, axis=0)
     numerator = jnp.sum(rescale * mixed, axis=0)
-    own_weight = [jnp.exp(own[0] - highest), jnp.where(second, jnp.exp(own[1] - highest), 0.0)]
+    own_weight = [
+        jnp.exp(own[0] - highest),
+        jnp.where(second_step, jnp.exp(own[1] - highest), 0.0),
+    ]
     for s in range(2):
         denominator = denominator + own_weight[s]
-        numerator = numerator + own_weight[s] * new_row(6 + kv, s)
-    attended = (numerator / denominator).astype(BF16).astype(F32)
-    att_all[pl.ds(mine, 8), :] = jnp.concatenate([attended, attended], axis=0)
-
-    @pl.loop(0, CTX - 1)
-    def _(i):
-        tile = att_all.at[pl.ds(mine, 8)]
-        send(3, tile, tile, (peer_of(x, z, i), t))
-
-    leaves(3, att_all.at[pl.ds(0, 8 * (CTX - 1))])
-
+        numerator = numerator + own_weight[s] * new_values[s]
+    mine = att_all.at[pl.ds(pl.multiple_of(request * 8, 8), 8)]
+    mine[...] = (numerator / denominator).astype(BF16).astype(F32)
+    for offset in far_first(NEAR):
+        if offset != (0, 0):
+            a, b = place(offset)
+            send(3, mine, mine, (a * 8 + b, t))
+
+    leaves(3, att_all.at[pl.ds(0, 8 * (REQS - 1))])
     loads[8].wait()
-    wait(recv_sem.at[3], att_all.at[pl.ds(0, 8 * (CTX - 1))])
+    wait(recv_sem.at[3], att_all.at[pl.ds(0, 8 * (REQS - 1))])
 
     att = jnp.concatenate(
         [
             jnp.concatenate(
                 [
-                    att_all[pl.ds((j // 2) * 8 + (j % 2) * 2 + s, REQS, stride=16), :]
+                    att_all[pl.ds(2 * j + s, REQS, stride=8), :]
                     for s in range(2)
                 ],
                 axis=0,
@@ -338,6 +395,9 @@
         def _(i):
             send(phase, proj_out.at[phase - 4], slots.at[t], (c, ring_peer(t, i)))
 
+        if phase == 5:
+            while left:
+                left.pop(0)()
         leaves(phase, slots.at[pl.ds(0, TEN - 1)])
 
         slots[t] = proj_out[phase - 4]
@@ -347,9 +407,9 @@
     residual = rows + over_tensor(4, nt_dot(att, wo[...]), proj_in)
 
     square = jnp.sum(residual * residual, axis=1, keepdims=True)
-    sq_out[...] = as_row(square)
-
-    sq_in[CTX - 1] = sq_out[...]
+    sq_out[0] = as_row(square)
+    along_x_all(6, sq_out.at[0], sqfx_in)
+
     loads[12].wait()
     loads[14].wait()
     ffn_gated = (residual * gain2[...].astype(F32)[None, :]).astype(BF16)
@@ -394,11 +454,8 @@
         for i in range(3):
             along_x(3 + n, k, i)
 
-    @pl.loop(0, CTX - 1)
-    def _(i):
-        send(6, sq_out, sq_in.at[i], (peer_of(x, z, i), t))
-
-    leaves(6, sq_in.at[pl.ds(0, CTX - 1)])
+    sq_out[1] = sum_of(6, sq_out.at[0], sqfx_in)
+    along_z_all(10, sq_out.at[1], sqfz_in)
 
     def x_sum(n, k):
         wait(gx_recv.at[n], gx_in.at[n])
@@ -460,8 +517,7 @@
     left.append(sent_extra)
     extra = (z < 2) | ((z == 2) & (x < 2))
 
-    wait(recv_sem.at[6], sq_in.at[pl.ds(0, CTX - 1)])
-    squares = jnp.sum(sq_in[...], axis=0)
+    squares = sum_of(10, sq_out.at[1], sqfz_in)
     step_rows = iota((REQS, HEAD), 1) == iota((REQS, HEAD), 0) + REQS * (x % 2)
     squares = jnp.sum(jnp.where(step_rows, squares, 0.0), axis=1, keepdims=True)
     ffn_inv = lax.rsqrt(squares / WIDTH + EPS)
@@ -477,52 +533,70 @@
         act = 0.5 * gate * (1.0 + jnp.tanh(GELU * (gate + 0.044715 * (gate * gate * gate))))
         return jnp.where(active, act * up, 0.0).astype(BF16)
 
-    def share(phase, unit):
-        part_of = hid_all.at[pl.ds(pl.multiple_of(unit * 16, 16), 16)]
+    owner = 4 * z + x
+
+    def units(first, count):
+        return hid_all.at[pl.ds(pl.multiple_of(first * 16, 16), count * 16)]
+
+    def share(first, count):
+        block = units(first, count)
 
         @pl.loop(0, CTX - 1)
         def _(i):
-            send(phase, part_of, part_of, (peer_of(x, z, i), t))
-
-    def unit_rows(unit):
-        return pl.ds(pl.multiple_of(unit * 16, 16), 16)
+            send(9, block, block, (peer_of(x, z, i), t))
 
     @pl.when(extra)
     def _():
         wait(recv_sem.at[8], gz_in2.at[pl.ds(0, 7)])
-        hid_all[unit_rows(32 + 4 * z + x), :] = hidden_of(gz_in2)
-        share(10, 32 + 4 * z + x)
+        units(2 * owner + 1, 1)[...] = hidden_of(gz_in2)
 
     wait(recv_sem.at[7], gz_in.at[pl.ds(0, 7)])
-    hid_all[unit_rows(4 * z + x), :] = hidden_of(gz_in)
-    share(9, 4 * z + x)
-    leaves(9, hid_all.at[pl.ds(0, 16 * (CTX - 1))])
-
-    def second_left():
+    hidden_main = hidden_of(gz_in)
+
+    @pl.when(extra)
+    def _():
+        units(2 * owner, 1)[...] = hidden_main
+        share(2 * owner, 2)
+
+    @pl.when(jnp.logical_not(extra))
+    def _():
+        units(owner + EXTRA, 1)[...] = hidden_main
+        share(owner + EXTRA, 1)
+
+    def hidden_left():
         @pl.when(extra)
         def _():
-            wait(send_sem.at[10], hid_all.at[pl.ds(0, 16 * (CTX - 1))])
-
-    left.append(second_left)
-
+            wait(send_sem.at[9], kc.at[0, pl.ds(0, 32 * (CTX - 1))])
+
+        @pl.when(jnp.logical_not(extra))
+        def _():
+            wait(send_sem.at[9], hid_all.at[pl.ds(0, 16 * (CTX - 1))])
+
+    left.append(hidden_left)
     loads[11].wait()
 
     @pl.when(extra)
     def _():
-        wait(recv_sem.at[10], hid_all.at[pl.ds(0, 16 * (EXTRA - 1))])
+        wait(recv_sem.at[9], hid_all.at[pl.ds(0, 16 * (CTX + EXTRA - 2))])
 
     @pl.when(jnp.logical_not(extra))
     def _():
-        wait(recv_sem.at[10], hid_all.at[pl.ds(0, 16 * EXTRA)])
-
-    wait(recv_sem.at[9], hid_all.at[pl.ds(0, 16 * (CTX - 1))])
+        wait(recv_sem.at[9], hid_all.at[pl.ds(0, 16 * (CTX + EXTRA - 1))])
+
+    def unit_at(unit):
+        own = unit % CTX
+        place = 2 * own + unit // CTX if own < EXTRA else own + EXTRA
+        return hid_all[place * 16 : place * 16 + 16, :]
+
     hidden = jnp.concatenate(
-        [hid_all[i * ROWS : (i + 1) * ROWS, :] for i in range(TILES)], axis=1
+        [
+            jnp.concatenate([unit_at(2 * i), unit_at(2 * i + 1)], axis=0)
+            for i in range(TILES)
+        ],
+        axis=1,
     )
     output = residual + over_tensor(5, nt_dot(hidden, wd[...]), down_in)
-    output = output.astype(BF16)
-    o1_ref[...] = output[0:REQS]
-    o2_ref[...] = output[REQS:ROWS]
+    out_ref[...] = output.astype(BF16)
 
     for sent in left:
         sent()
@@ -548,14 +622,13 @@
     hbm = pl.BlockSpec(memory_space=pltpu.HBM)
     vmem = pl.BlockSpec(memory_space=pltpu.VMEM)
     V = pltpu.VMEM
-    return pl.pallas_call(
+    (both,) = pl.pallas_call(
         kernel,
         out_shape=(
-            pltpu.VMEM((REQS, COLS), BF16),
-            pltpu.VMEM((REQS, COLS), BF16),
+            pltpu.VMEM((ROWS, COLS), BF16),
         ),
         in_specs=[hbm] * 15,
-        out_specs=(vmem, vmem),
+        out_specs=(vmem,),
         scratch_shapes=[
             pltpu.SMEM((REQS,), jnp.int32),
             pltpu.SMEM((REQS,), jnp.int32),
@@ -575,20 +648,21 @@
             V((4, REQS, 512), BF16),
             V((2, 3, REQS, 512), BF16),
             V((2, 7, REQS, 512), BF16),
-            V((2, ROWS, 512), BF16),
-            V((3, ROWS, 512), BF16),
-            V((7, ROWS, 512), BF16),
+            V((REQS * 8, HEAD), F32),
+            V((CTX, 8, HEAD), F32),
+            V((ROWS, HEAD), F32),
             V((2, 1, HEAD), F32),
             V((3, 1, HEAD), F32),
             V((7, 1, HEAD), F32),
-            V((CTX * 8, HEAD), F32),
-            V((CTX, 8, HEAD), F32),
-            V((CTX, 8, HEAD), F32),
-            V((CTX * 8, HEAD), F32),
+            V((REQS * 8, HEAD), F32),
+            V((REQS, 16, HEAD), BF16),
+            V((CTX, 16, HEAD), BF16),
+            V((REQS * 8, HEAD), F32),
             V((2, ROWS, 2 * HEAD), BF16),
             V((TEN, ROWS, 2 * HEAD), BF16),
-            V((1, HEAD), F32),
-            V((CTX, 1, HEAD), F32),
+            V((2, 1, HEAD), F32),
+            V((3, 1, HEAD), F32),
+            V((7, 1, HEAD), F32),
             V((2 * TILES, 32, HEAD), BF16),
             V((11, 3, 32, HEAD), BF16),
             V((10, 32, HEAD), BF16),
@@ -623,6 +697,7 @@
         key_cache.reshape(REQS, 2 * POS, HEAD),
         value_cache.reshape(REQS, 2 * POS, HEAD),
     )
+    return both[0:REQS], both[REQS:ROWS]
 
 
 def solution(mesh):

time: 62.7 us -> 58.6 us (0.935)
  Pallas kernels: 60.7 us -> 57.2 us
    pallas_call x1, Pallas kernels: 60.7 us -> 57.2 us  [per_device(): pl.pallas_call(kernel, out_shape=(pltpu.VMEM((ROWS, COLS), BF16),), in_sp...]
    unnamed x2 -> x0, local copies, waits for them, and re-layouts: 1.2 us -> none
where the time goes in v4:
time: 58.6 us; the launch traced here: 58.5 us
  Pallas kernels  57.2 us (98%)
  between operations  0.64 us (1%)
  local copies, waits for them, and re-layouts  0.61 us (1%)
    pallas_call x1, Pallas kernels, per_device(): pl.pallas_call(kernel, out_shape=(pltpu.VMEM((ROWS, COLS), BF16),), in_sp...  57.2 us

profile of v4, /device:TPU:1, one launch (start us, length us, event | category | flops | bytes accessed | tf_op | source)
XLA Modules:
  0.0 58.5 jit_solution(10438617084249926345)
XLA Ops:
  0.6 57.2 %shard_map.158 = bf16[32,168]{1,0:T(8,128)(2,1)S(1)} custom-call(s32[16]{0:T(128)} %lengths_hbm.1, s32[16]{0:T(128)} %granularity_hbm.1, bf16[16,168]{1,0:T(8,128)(2,1)} %x1_hbm.1, bf16[16,168]{1,0:T(8,128)(2,1)} %x2_hbm.1, bf16[168]{0:T(256)(128)(2,1)} %gain1_hbm.1, bf16[168]{0:T(256)(128)(2,1)} %gain2_hbm.1, bf16[168,512]{1,0:T(8,128)(2,1)} %wq_hbm.1, ...), custom_call_target="tpu_custom_call" | custom-call | tf_op jit(solution)/shard_map/pallas_call | solution.py:625
  57.8 0.6 %fusion = (bf16[16,168]{1,0:T(8,128)(2,1)}, bf16[16,168]{1,0:T(8,128)(2,1)}) fusion(bf16[32,168]{1,0:T(8,128)(2,1)S(1)} %shard_map.158), kind=kLoop, calls=%fused_computation | loop fusion | bytes 21504 | tf_op jit(solution)/shard_map/slice | solution.py:700

commit v5 on v4

--- a/solution.py
+++ b/solution.py
@@ -106,11 +106,17 @@
     wd,
     kc,
     vc,
-    q_out,
-    qx_in,
-    qz_in,
+    qa_out,
+    qb_out,
+    qax_in,
+    qaz_in,
+    qbz_in,
+    qbx_in,
+    kv_part_rows,
     kv_out,
-    kv_in,
+    kvx_in,
+    kv_sum,
+    kvz_in,
     inv_rows,
     new_sq,
     sqx_in,
@@ -213,8 +219,8 @@
     q_part = jnp.dot(gated, wq[...], preferred_element_type=F32)
     k_part = jnp.dot(gated, wk[...], preferred_element_type=F32)
     v_part = jnp.dot(gated, wv[...], preferred_element_type=F32)
-    q_out[0] = q_part[0:REQS].astype(BF16)
-    q_out[1] = q_part[REQS:ROWS].astype(BF16)
+    qa_out[0] = q_part[0:REQS].astype(BF16)
+    qb_out[0] = q_part[REQS:ROWS].astype(BF16)
     diagonal = iota((ROWS, HEAD), 0) == iota((ROWS, HEAD), 1)
 
     def as_row(column):
@@ -245,42 +251,55 @@
         wait(recv_sem.at[phase], slots)
         return own[...].astype(F32) + jnp.sum(slots[...].astype(F32), axis=0)
 
-    along_z_all(1, q_out.at[1], qz_in.at[1])
-    along_x_all(0, q_out.at[0], qx_in.at[0])
+    def place(offset):
+        return lax.rem(x + offset[0], 4), lax.rem(z + offset[1], 8)
+
+    def request_at(at):
+        return (at[0] % 2) * 8 + lax.rem(at[1] + 4 * (at[0] // 2), 8)
+
+    along_z_all(1, qb_out.at[0], qbz_in)
+    along_x_all(0, qa_out.at[0], qax_in)
     along_x_all(11, new_sq.at[0], sqx_in)
+
     kv_part = jnp.concatenate([k_part, v_part], axis=1)
     for s in range(2):
         for j in range(4):
-            kv_out[pl.ds(4 * s + j, REQS, stride=8), :] = kv_part[
+            kv_part_rows[pl.ds(4 * s + j, REQS, stride=8), :] = kv_part[
                 s * REQS : s * REQS + REQS, j * HEAD : (j + 1) * HEAD
             ]
+    for parity in range(2):
+        kv_out[parity] = kv_part_rows[64 * parity : 64 * parity + 64, :].astype(BF16)
+
+    @pl.loop(0, 3)
+    def _(i):
+        a = ring_peer(x, i, 4)
+        send(12, kv_out.at[a % 2], kvx_in.at[i], (a * 8 + z, t))
+
+    leaves(12, kvx_in)
+    qa_out[1] = sum_of(0, qa_out.at[0], qax_in).astype(BF16)
+    along_z_all(13, qa_out.at[1], qaz_in)
     new_sq[1] = sum_of(11, new_sq.at[0], sqx_in)
-    q_out[2] = sum_of(0, q_out.at[0], qx_in.at[0]).astype(BF16)
-    along_z_all(13, q_out.at[2], qz_in.at[0])
     along_z_all(14, new_sq.at[1], sqz_in)
-    q_out[3] = sum_of(1, q_out.at[1], qz_in.at[1]).astype(BF16)
-    along_x_all(15, q_out.at[3], qx_in.at[1])
+    qb_out[1] = sum_of(1, qb_out.at[0], qbz_in).astype(BF16)
+    along_x_all(15, qb_out.at[1], qbx_in)
+    kv_sum[...] = sum_of(12, kv_out.at[x % 2], kvx_in)
+
+    def kv_rows(place_z):
+        local_request = lax.rem(place_z + 4 * (x // 2), 8)
+        return kv_sum.at[pl.ds(pl.multiple_of(local_request * 8, 8), 8)]
+
+    @pl.loop(0, 7)
+    def _(i):
+        b = ring_peer(z, i)
+        send(16, kv_rows(b), kvz_in.at[i], (x * 8 + b, t))
+
+    leaves(16, kvz_in)
     squares = as_column(sum_of(14, new_sq.at[1], sqz_in))
     inv = lax.rsqrt(squares / WIDTH + EPS)
     inv_rows[...] = jnp.broadcast_to(inv, (ROWS, HEAD))
-    second_total = sum_of(15, q_out.at[3], qx_in.at[1])
-
-    def place(offset):
-        return lax.rem(x + offset[0], 4), lax.rem(z + offset[1], 8)
-
-    def request_at(at):
-        return (at[0] % 2) * 8 + lax.rem(at[1] + 4 * (at[0] // 2), 8)
-
-    def request_rows(ref, r):
-        return ref.at[pl.ds(pl.multiple_of(r * 8, 8), 8)]
-
-    for offset in far_first(NEAR + [opposite(offset) for offset in NEAR]):
-        if offset != (0, 0):
-            a, b = place(offset)
-            send(12, request_rows(kv_out, request_at((a, b))), kv_in.at[c], (a * 8 + b, t))
-
-    leaves(12, kv_in.at[pl.ds(0, CTX - 1)])
-    totals = [sum_of(13, q_out.at[2], qz_in.at[0]), second_total]
+    part_b = sum_of(15, qb_out.at[1], qbx_in)
+    part_a = sum_of(13, qa_out.at[1], qaz_in)
+    totals = [part_a, part_b]
     for s in range(2):
         query = (totals[s] * inv[s * REQS : s * REQS + REQS]).astype(BF16).astype(F32)
         for j in range(4):
@@ -330,13 +349,11 @@
 
     request = request_at((x, z))
     mix_in[c] = mix_out[request]
-    kv_in[c] = request_rows(kv_out, request)[...]
     query = qkv_all[pl.ds(request, 8, stride=16), :]
     first_head = iota((8, 1), 0) < 4
     second_step = (iota((8, 1), 0) % 2) == 1
     inv_step = [inv_rows[pl.ds(s * REQS + request, 1), :] for s in range(2)]
-    wait(recv_sem.at[12], kv_in.at[pl.ds(0, CTX - 1)])
-    new = jnp.sum(kv_in[...], axis=0) * jnp.where(first_head, inv_step[0], inv_step[1])
+    new = sum_of(16, kv_rows(z), kvz_in) * jnp.where(first_head, inv_step[0], inv_step[1])
     new = new.astype(BF16).astype(F32)
 
     def new_rows(j, s):
@@ -436,86 +453,87 @@
             device_id_type=MESH,
         ).start()
 
-    for n in range(3):
-        partial(8 + n, 2 if n < 2 else 1)
-        for i in range(3):
-            if n < 2:
-                along_x(n, 8 + n, i)
-            else:
-
-                @pl.when(ring_peer(x, i, 4) < 2)
-                def _():
-                    along_x(2, 10, i)
-
     @pl.loop(0, 8)
     def _(n):
         k = ring_peer(z, n)
         partial(k, 2)
         for i in range(3):
-            along_x(3 + n, k, i)
+            along_x(k, k, i)
+
+        @pl.when(k < 2)
+        def _():
+            partial(8 + k, 2)
+            for i in range(3):
+                along_x(8 + k, 8 + k, i)
+
+        @pl.when(k == 2)
+        def _():
+            partial(10, 1)
+            for i in range(3):
+
+                @pl.when(ring_peer(x, i, 4) < 2)
+                def _():
+                    along_x(10, 10, i)
 
     sq_out[1] = sum_of(6, sq_out.at[0], sqfx_in)
     along_z_all(10, sq_out.at[1], sqfz_in)
 
-    def x_sum(n, k):
-        wait(gx_recv.at[n], gx_in.at[n])
+    def x_sum(k):
+        wait(gx_recv.at[k], gx_in.at[k])
         total = gu_out[4 * k + x].astype(F32)
         for i in range(3):
-            total = total + gx_in[n, i].astype(F32)
+            total = total + gx_in[k, i].astype(F32)
         return total.astype(BF16)
 
-    for n in range(3):
-        here = (x < 4) if n < 2 else (x < 2)
-
-        @pl.when(here & (z == n))
-        def _():
-            gz_in2[z] = x_sum(n, 8 + n)
-
-        @pl.when(here & (z != n))
-        def _():
-            gz_out[n] = x_sum(n, 8 + n)
-            pltpu.make_async_remote_copy(
-                src_ref=gz_out.at[n],
-                dst_ref=gz_in2.at[z],
-                send_sem=gz_send.at[n],
-                recv_sem=recv_sem.at[8],
-                device_id=(x * 8 + n, t),
-                device_id_type=MESH,
-            ).start()
+    def to_owner(k, slot, send_from, recv_at):
+        pltpu.make_async_remote_copy(
+            src_ref=gz_out.at[k],
+            dst_ref=slot,
+            send_sem=send_from,
+            recv_sem=recv_at,
+            device_id=(x * 8 + k % 8, t),
+            device_id_type=MESH,
+        ).start()
 
     @pl.loop(0, 7)
     def _(n):
         k = ring_peer(z, n)
-        gz_out[3 + n] = x_sum(3 + n, k)
-        send(7, gz_out.at[3 + n], gz_in.at[n], (x * 8 + k, t))
-
-    gz_in[7] = x_sum(10, z)
+        gz_out[k] = x_sum(k)
+        to_owner(k, gz_in.at[n], send_sem.at[7], recv_sem.at[7])
+
+        @pl.when((k < 2) | ((k == 2) & (x < 2)))
+        def _():
+            gz_out[8 + k] = x_sum(8 + k)
+            to_owner(8 + k, gz_in2.at[n], gz_send.at[k], recv_sem.at[8])
+
+    gz_in[7] = x_sum(z)
     leaves(7, gz_in.at[pl.ds(0, 7)])
+    extra = (z < 2) | ((z == 2) & (x < 2))
+
+    @pl.when(extra)
+    def _():
+        gz_in2[7] = x_sum(8 + z)
 
     def sent_extra():
-        for n in range(3):
-            if n < 2:
-                wait(gx_send.at[n], gx_in.at[n])
-            else:
-
-                @pl.when(x < 2)
-                def _():
-                    wait(gx_send.at[n], gx_in.at[n, pl.ds(0, 1)])
-
-                @pl.when(x >= 2)
-                def _():
-                    wait(gx_send.at[n], gx_in.at[n, pl.ds(0, 2)])
-
-            @pl.when(((x < 4) if n < 2 else (x < 2)) & (z != n))
+        @pl.loop(0, 10)
+        def _(k):
+            wait(gx_send.at[k], gx_in.at[k])
+
+        @pl.when(x < 2)
+        def _():
+            wait(gx_send.at[10], gx_in.at[10, pl.ds(0, 1)])
+
+        @pl.when(x >= 2)
+        def _():
+            wait(gx_send.at[10], gx_in.at[10, pl.ds(0, 2)])
+
+        for k in range(3):
+
+            @pl.when(((x < 4) if k < 2 else (x < 2)) & (z != k))
             def _():
-                wait(gz_send.at[n], gz_out.at[n])
-
-        @pl.loop(3, 11)
-        def _(n):
-            wait(gx_send.at[n], gx_in.at[n])
+                wait(gz_send.at[k], gz_out.at[8 + k])
 
     left.append(sent_extra)
-    extra = (z < 2) | ((z == 2) & (x < 2))
 
     squares = sum_of(10, sq_out.at[1], sqfz_in)
     step_rows = iota((REQS, HEAD), 1) == iota((REQS, HEAD), 0) + REQS * (x % 2)
@@ -645,11 +663,17 @@
             V((COLS, 2688), BF16),
             V((REQS, 2 * POS, HEAD), BF16),
             V((REQS, 2 * POS, HEAD), BF16),
-            V((4, REQS, 512), BF16),
-            V((2, 3, REQS, 512), BF16),
-            V((2, 7, REQS, 512), BF16),
+            V((2, REQS, 512), BF16),
+            V((2, REQS, 512), BF16),
+            V((3, REQS, 512), BF16),
+            V((7, REQS, 512), BF16),
+            V((7, REQS, 512), BF16),
+            V((3, REQS, 512), BF16),
             V((REQS * 8, HEAD), F32),
-            V((CTX, 8, HEAD), F32),
+            V((2, 64, HEAD), BF16),
+            V((3, 64, HEAD), BF16),
+            V((64, HEAD), F32),
+            V((7, 8, HEAD), F32),
             V((ROWS, HEAD), F32),
             V((2, 1, HEAD), F32),
             V((3, 1, HEAD), F32),
@@ -665,7 +689,7 @@
             V((7, 1, HEAD), F32),
             V((2 * TILES, 32, HEAD), BF16),
             V((11, 3, 32, HEAD), BF16),
-            V((10, 32, HEAD), BF16),
+            V((11, 32, HEAD), BF16),
             V((8, 32, HEAD), BF16),
             V((8, 32, HEAD), BF16),
             V((TILES * ROWS, HEAD), BF16),

time: 58.6 us -> 57.6 us (0.983)
  Pallas kernels: 57.2 us -> 56.2 us
    pallas_call x1, Pallas kernels: 57.2 us -> 56.2 us  [per_device(): pl.pallas_call(kernel, out_shape=(pltpu.VMEM((ROWS, COLS), BF16),), in_sp...]
where the time goes in v5:
time: 57.6 us; the launch traced here: 57.5 us
  Pallas kernels  56.2 us (98%)
  between operations  0.64 us (1%)
  local copies, waits for them, and re-layouts  0.61 us (1%)
    pallas_call x1, Pallas kernels, per_device(): pl.pallas_call(kernel, out_shape=(pltpu.VMEM((ROWS, COLS), BF16),), in_sp...  56.2 us

profile of v5, /device:TPU:1, one launch (start us, length us, event | category | flops | bytes accessed | tf_op | source)
XLA Modules:
  0.0 57.5 jit_solution(8206138927369176959)
XLA Ops:
  0.6 56.2 %shard_map.158 = bf16[32,168]{1,0:T(8,128)(2,1)S(1)} custom-call(s32[16]{0:T(128)} %lengths_hbm.1, s32[16]{0:T(128)} %granularity_hbm.1, bf16[16,168]{1,0:T(8,128)(2,1)} %x1_hbm.1, bf16[16,168]{1,0:T(8,128)(2,1)} %x2_hbm.1, bf16[168]{0:T(256)(128)(2,1)} %gain1_hbm.1, bf16[168]{0:T(256)(128)(2,1)} %gain2_hbm.1, bf16[168,512]{1,0:T(8,128)(2,1)} %wq_hbm.1, ...), custom_call_target="tpu_custom_call" | custom-call | tf_op jit(solution)/shard_map/pallas_call | solution.py:643
  56.8 0.6 %fusion = (bf16[16,168]{1,0:T(8,128)(2,1)}, bf16[16,168]{1,0:T(8,128)(2,1)}) fusion(bf16[32,168]{1,0:T(8,128)(2,1)S(1)} %shard_map.158), kind=kLoop, calls=%fused_computation | loop fusion | bytes 21504 | tf_op jit(solution)/shard_map/slice | solution.py:724

commit v6 on v5

--- a/solution.py
+++ b/solution.py
@@ -257,9 +257,9 @@
     def request_at(at):
         return (at[0] % 2) * 8 + lax.rem(at[1] + 4 * (at[0] // 2), 8)
 
+    along_x_all(11, new_sq.at[0], sqx_in)
+    along_x_all(0, qa_out.at[0], qax_in)
     along_z_all(1, qb_out.at[0], qbz_in)
-    along_x_all(0, qa_out.at[0], qax_in)
-    along_x_all(11, new_sq.at[0], sqx_in)
 
     kv_part = jnp.concatenate([k_part, v_part], axis=1)
     for s in range(2):
@@ -276,10 +276,10 @@
         send(12, kv_out.at[a % 2], kvx_in.at[i], (a * 8 + z, t))
 
     leaves(12, kvx_in)
+    new_sq[1] = sum_of(11, new_sq.at[0], sqx_in)
+    along_z_all(14, new_sq.at[1], sqz_in)
     qa_out[1] = sum_of(0, qa_out.at[0], qax_in).astype(BF16)
     along_z_all(13, qa_out.at[1], qaz_in)
-    new_sq[1] = sum_of(11, new_sq.at[0], sqx_in)
-    along_z_all(14, new_sq.at[1], sqz_in)
     qb_out[1] = sum_of(1, qb_out.at[0], qbz_in).astype(BF16)
     along_x_all(15, qb_out.at[1], qbx_in)
     kv_sum[...] = sum_of(12, kv_out.at[x % 2], kvx_in)

time: 57.6 us -> 56.8 us (0.986)
  Pallas kernels: 56.2 us -> 55.4 us
    pallas_call x1, Pallas kernels: 56.2 us -> 55.4 us  [per_device(): pl.pallas_call(kernel, out_shape=(pltpu.VMEM((ROWS, COLS), BF16),), in_sp...]
where the time goes in v6:
time: 56.8 us; the launch traced here: 56.6 us
  Pallas kernels  55.4 us (98%)
  between operations  0.64 us (1%)
  local copies, waits for them, and re-layouts  0.61 us (1%)
    pallas_call x1, Pallas kernels, per_device(): pl.pallas_call(kernel, out_shape=(pltpu.VMEM((ROWS, COLS), BF16),), in_sp...  55.4 us

profile of v6, /device:TPU:1, one launch (start us, length us, event | category | flops | bytes accessed | tf_op | source)
XLA Modules:
  0.0 56.6 jit_solution(16821746796945505453)
XLA Ops:
  0.6 55.4 %shard_map.158 = bf16[32,168]{1,0:T(8,128)(2,1)S(1)} custom-call(s32[16]{0:T(128)} %lengths_hbm.1, s32[16]{0:T(128)} %granularity_hbm.1, bf16[16,168]{1,0:T(8,128)(2,1)} %x1_hbm.1, bf16[16,168]{1,0:T(8,128)(2,1)} %x2_hbm.1, bf16[168]{0:T(256)(128)(2,1)} %gain1_hbm.1, bf16[168]{0:T(256)(128)(2,1)} %gain2_hbm.1, bf16[168,512]{1,0:T(8,128)(2,1)} %wq_hbm.1, ...), custom_call_target="tpu_custom_call" | custom-call | tf_op jit(solution)/shard_map/pallas_call | solution.py:643
  56.0 0.6 %fusion = (bf16[16,168]{1,0:T(8,128)(2,1)}, bf16[16,168]{1,0:T(8,128)(2,1)}) fusion(bf16[32,168]{1,0:T(8,128)(2,1)S(1)} %shard_map.158), kind=kLoop, calls=%fused_computation | loop fusion | bytes 21504 | tf_op jit(solution)/shard_map/slice | solution.py:724

commit v7 on v6

--- a/solution.py
+++ b/solution.py
@@ -106,6 +106,7 @@
     wd,
     kc,
     vc,
+    kt,
     qa_out,
     qb_out,
     qax_in,
@@ -280,6 +281,14 @@
     along_z_all(14, new_sq.at[1], sqz_in)
     qa_out[1] = sum_of(0, qa_out.at[0], qax_in).astype(BF16)
     along_z_all(13, qa_out.at[1], qaz_in)
+
+    def transpose_keys(first):
+        @pl.loop(first, first + 8)
+        def _(r):
+            kt[r] = kc[r].T
+
+    loads[6].wait()
+    transpose_keys(0)
     qb_out[1] = sum_of(1, qb_out.at[0], qbz_in).astype(BF16)
     along_x_all(15, qb_out.at[1], qbx_in)
     kv_sum[...] = sum_of(12, kv_out.at[x % 2], kvx_in)
@@ -294,6 +303,7 @@
         send(16, kv_rows(b), kvz_in.at[i], (x * 8 + b, t))
 
     leaves(16, kvz_in)
+    transpose_keys(8)
     squares = as_column(sum_of(14, new_sq.at[1], sqz_in))
     inv = lax.rsqrt(squares / WIDTH + EPS)
     inv_rows[...] = jnp.broadcast_to(inv, (ROWS, HEAD))
@@ -307,7 +317,6 @@
             qkv_all[start : start + REQS, :] = query[:, j * HEAD : (j + 1) * HEAD]
 
     loads[13].wait()
-    loads[6].wait()
     loads[7].wait()
     lane = iota((8, 2 * POS), 1)
     own_head = (lane % 2) == (iota((8, 2 * POS), 0) // 4)
@@ -317,7 +326,7 @@
     for half in (NEAR[:8], NEAR[8:]):
         requests = [request_at(place(offset)) for offset in half]
         queries = [qkv_all[pl.ds(r, 8, stride=16), :].astype(BF16) for r in requests]
-        scores = [nt_dot(q, kc[r]) * SCALE for q, r in zip(queries, requests)]
+        scores = [jnp.dot(q, kt[r], preferred_element_type=F32) * SCALE for q, r in zip(queries, requests)]
         live = [own_head & (position < lengths[r]) for r in requests]
         peaks = [
             jnp.max(jnp.where(l, s, MASKED), axis=1, keepdims=True) for s, l in zip(scores, live)
@@ -663,6 +672,7 @@
             V((COLS, 2688), BF16),
             V((REQS, 2 * POS, HEAD), BF16),
             V((REQS, 2 * POS, HEAD), BF16),
+            V((REQS, HEAD, 2 * POS), BF16),
             V((2, REQS, 512), BF16),
             V((2, REQS, 512), BF16),
             V((3, REQS, 512), BF16),

time: 56.8 us -> 56.3 us (level)
  no operation moved by 1% of the time
where the time goes in v7:
time: 56.3 us; the launch traced here: 56.1 us
  Pallas kernels  54.9 us (98%)
  between operations  0.64 us (1%)
  local copies, waits for them, and re-layouts  0.61 us (1%)
    pallas_call x1, Pallas kernels, per_device(): pl.pallas_call(kernel, out_shape=(pltpu.VMEM((ROWS, COLS), BF16),), in_sp...  54.9 us

profile of v7, /device:TPU:1, one launch (start us, length us, event | category | flops | bytes accessed | tf_op | source)
XLA Modules:
  0.0 56.1 jit_solution(10091816456573681219)
XLA Ops:
  0.6 54.9 %shard_map.158 = bf16[32,168]{1,0:T(8,128)(2,1)S(1)} custom-call(s32[16]{0:T(128)} %lengths_hbm.1, s32[16]{0:T(128)} %granularity_hbm.1, bf16[16,168]{1,0:T(8,128)(2,1)} %x1_hbm.1, bf16[16,168]{1,0:T(8,128)(2,1)} %x2_hbm.1, bf16[168]{0:T(256)(128)(2,1)} %gain1_hbm.1, bf16[168]{0:T(256)(128)(2,1)} %gain2_hbm.1, bf16[168,512]{1,0:T(8,128)(2,1)} %wq_hbm.1, ...), custom_call_target="tpu_custom_call" | custom-call | tf_op jit(solution)/shard_map/pallas_call | solution.py:652
  55.5 0.6 %fusion = (bf16[16,168]{1,0:T(8,128)(2,1)}, bf16[16,168]{1,0:T(8,128)(2,1)}) fusion(bf16[32,168]{1,0:T(8,128)(2,1)S(1)} %shard_map.158), kind=kLoop, calls=%fused_computation | loop fusion | bytes 21504 | tf_op jit(solution)/shard_map/slice | solution.py:734
